TPU v7x, 32 devices: a whole 2x2x4 slice. The times are simulated.
32 devices in a mesh: page: 4 (over z), blk: 8 (over y, x, core).
Axes of the slice: x: 2, y: 2, z: 4, core: 2. Of those that a mesh axis runs over, the one named last changes fastest.
Arguments:
- tokens: bfloat16 [8, 4096, 1024], P('page', 'blk'), may hold values from -6 to 6
- memory: bfloat16 [8, 588, 1024], P('page', None, 'blk'), may hold values from -6 to 6
- end_only: int32 [8], P('page'), may hold values from 0 to 1, as said below
- lengths: int32 [8], P('page'), may hold values from 1 to 4096, as said below
- norm_gain: float32 [3, 1024], replicated, may hold values from 0.5 to 1.5
- norm_bias: float32 [3, 1024], replicated, may hold values from -3 to 3
- self_qkv: bfloat16 [1024, 3072], replicated, may hold values from -0.1875 to 0.1875
- self_out: bfloat16 [1024, 1024], replicated, may hold values from -1.5 to 1.5
- cross_q: bfloat16 [1024, 1024], replicated, may hold values from -0.1875 to 0.1875
- cross_kv: bfloat16 [1024, 2048], replicated, may hold values from -0.1875 to 0.1875
- cross_out: bfloat16 [1024, 1024], replicated, may hold values from -1.5 to 1.5
- fc_in: bfloat16 [1024, 4096], replicated, may hold values from -0.1875 to 0.1875
- fc_out: bfloat16 [4096, 1024], replicated, may hold values from -0.09375 to 0.09375
- fc_in_bias: float32 [4096], replicated, may hold values from -3 to 3
- proj_bias: float32 [7, 1024], replicated, may hold values from -3 to 3
- cotangent: bfloat16 [8, 4096, 1024], P('page', 'blk'), may hold values from -6 to 6
Outputs:
- out: bfloat16 [8, 4096, 1024], P('page', 'blk')
- grad_tokens: float32 [8, 4096, 1024], P('page', 'blk')
- grad_memory: float32 [8, 588, 1024], P('page', None, 'blk')
- grad_norm_gain: float32 [3, 1024], P(None, 'blk')
- grad_norm_bias: float32 [3, 1024], P(None, 'blk')
- grad_self_qkv: float32 [1024, 3072], P('blk')
- grad_self_out: float32 [1024, 1024], P('blk')
- grad_cross_q: float32 [1024, 1024], P('blk')
- grad_cross_kv: float32 [1024, 2048], P('blk')
- grad_cross_out: float32 [1024, 1024], P('blk')
- grad_fc_in: float32 [1024, 4096], P('blk')
- grad_fc_out: float32 [4096, 1024], P('blk')
- grad_fc_in_bias: float32 [4096], P('blk')
- grad_proj_bias: float32 [7, 1024], P(None, 'blk')
Inputs may be any that keep to these rules, and one draw needn't show every extreme that they name: `lengths`: in each group of 2 consecutive sequences one has length 4096 and end_only 0. At least one sequence of the whole batch has end_only 1.
All inputs are finite; a program needn't handle non-finite values.
Results may differ from a plain program's by a relative error of at most 0.02.
Values may be sent and summed in bfloat16 or wider, within the bound.
No kernel may reach another device: no remote copies, remote signals or barrier semaphores. Data moves between devices by JAX's collectives and lax.ppermute only.
A program may use at most 576 MiB of HBM per device.

v0:
```python
from functools import partial

import jax
import jax.numpy as jnp
from jax import lax
from jax.sharding import PartitionSpec as P

HEADS = 16


EPSILON = 1e-05
NEG_LARGE = -1e30
HALF_TYPE = jnp.bfloat16
head_group = 4


def layer_norm(vector, gain_vec, shift_vec):
    centre = vector - jnp.mean(vector, axis=-1, keepdims=True)
    spread = jnp.mean(centre * centre, axis=-1, keepdims=True)
    return centre * lax.rsqrt(spread + EPSILON) * gain_vec + shift_vec


def product(left_op, right_op):
    return jnp.dot(left_op, right_op, preferred_element_type=jnp.float32)


def col_sums(tensor):
    return jnp.sum(tensor.astype(jnp.float32), axis=0)


def to_heads(tensor):
    n_seq, n_rows, n_feat = tensor.shape
    split = tensor.reshape(n_seq, n_rows, HEADS, n_feat // HEADS).transpose(0, 2, 1, 3)
    return split.reshape(n_seq * HEADS, n_rows, n_feat // HEADS)


def from_heads(tensor, n_seq):
    stacked, n_rows, head_width = tensor.shape
    joined = tensor.reshape(n_seq, HEADS, n_rows, head_width).transpose(0, 2, 1, 3)
    return joined.reshape(n_seq, n_rows, HEADS * head_width)


def grouped(tensor):
    return tensor.reshape((tensor.shape[0] // head_group, head_group) + tensor.shape[1:])


def ungrouped(tensor):
    return tensor.reshape((tensor.shape[0] * tensor.shape[1],) + tensor.shape[2:])


def run_heads(function, inputs):
    return jax.tree.map(ungrouped, lax.map(function, jax.tree.map(grouped, inputs)))


def raw_scores(queries, key_rows, offset):
    scores = (
        jnp.einsum("gqd,gkd->gqk", queries, key_rows, preferred_element_type=jnp.float32) * 0.125
    )
    if offset is None:
        return scores
    query_pos = offset + jnp.arange(queries.shape[1], dtype=jnp.int32)[:, None]
    key_pos = jnp.arange(key_rows.shape[1], dtype=jnp.int32)[None, :]
    return jnp.where((key_pos <= query_pos)[None], scores, NEG_LARGE)


def head_forward(offset, inputs):
    queries, key_rows, values = inputs
    scores = raw_scores(queries, key_rows, offset)
    row_max = jnp.max(scores, axis=-1, keepdims=True)
    exp_scores = jnp.exp(scores - row_max)
    row_sum = jnp.sum(exp_scores, axis=-1, keepdims=True)
    attn_probs = (exp_scores / row_sum).astype(HALF_TYPE)
    result = jnp.einsum("gqk,gkd->gqd", attn_probs, values, preferred_element_type=jnp.float32)
    return (result, row_max[..., 0], row_sum[..., 0])


def head_backward(offset, inputs):
    queries, key_rows, values, grad_out, row_max, row_sum = inputs
    scores = raw_scores(queries, key_rows, offset)
    attn_probs = jnp.exp(scores - row_max[..., None]) / row_sum[..., None]
    grad_probs = jnp.einsum("gqd,gkd->gqk", grad_out, values, preferred_element_type=jnp.float32)
    row_delta = jnp.sum(attn_probs * grad_probs, axis=-1, keepdims=True)
    grad_scores = (attn_probs * (grad_probs - row_delta)).astype(HALF_TYPE)
    grad_query = (
        jnp.einsum("gqk,gkd->gqd", grad_scores, key_rows, preferred_element_type=jnp.float32)
        * 0.125
    )
    grad_key = (
        jnp.einsum("gqk,gqd->gkd", grad_scores, queries, preferred_element_type=jnp.float32) * 0.125
    )
    grad_value = jnp.einsum(
        "gqk,gqd->gkd", attn_probs.astype(HALF_TYPE), grad_out, preferred_element_type=jnp.float32
    )
    return (grad_query, grad_key, grad_value)


def shards(
    tokens,
    memory,
    end_only,
    lengths,
    norm_gain,
    norm_bias,
    self_qkv,
    self_out,
    cross_q,
    cross_kv,
    cross_out,
    fc_in,
    fc_out,
    fc_in_bias,
    proj_bias,
    cotangent,
):
    local_seqs, local_rows, model_width = tokens.shape
    mem_count = memory.shape[1]
    shard_width = memory.shape[2]
    block_index = lax.axis_index("blk")
    offset = block_index * local_rows
    flat_rows = local_seqs * local_rows
    live_span = jnp.where(end_only == 1, 1, lengths)
    positions = offset + jnp.arange(local_rows, dtype=jnp.int32)
    row_valid = (positions[None, :] < live_span[:, None]).astype(jnp.float32)
    row_mask = row_valid.reshape(flat_rows, 1)
    stream_in = tokens.astype(jnp.float32).reshape(flat_rows, model_width)
    normed_self = layer_norm(stream_in, norm_gain[0], norm_bias[0]).astype(HALF_TYPE)
    projected = product(normed_self, self_qkv)
    queries = (projected[:, :model_width] + proj_bias[0]).astype(HALF_TYPE)
    key_val = jnp.concatenate(
        [
            projected[:, model_width : 2 * model_width],
            projected[:, 2 * model_width :] + proj_bias[1],
        ],
        axis=1,
    ).astype(HALF_TYPE)
    key_val = key_val.reshape(local_seqs, local_rows, 2 * model_width)
    kv_whole = lax.all_gather(key_val, "blk", axis=1, tiled=True)
    query_heads = to_heads(queries.reshape(local_seqs, local_rows, model_width))
    key_heads = to_heads(kv_whole[:, :, :model_width])
    value_heads = to_heads(kv_whole[:, :, model_width:])
    self_result, self_max, self_sum = run_heads(
        partial(head_forward, offset), (query_heads, key_heads, value_heads)
    )
    attended = from_heads(self_result, local_seqs).reshape(flat_rows, model_width).astype(HALF_TYPE)
    stream_mid = stream_in + product(attended, self_out) + proj_bias[2]
    normed_cross = layer_norm(stream_mid, norm_gain[1], norm_bias[1]).astype(HALF_TYPE)
    cross_queries = (product(normed_cross, cross_q) + proj_bias[3]).astype(HALF_TYPE)
    own_rows = lax.dynamic_slice_in_dim(cross_kv, block_index * shard_width, shard_width, 0)
    mem_share = memory.reshape(local_seqs * mem_count, shard_width)
    whole_memory = lax.all_gather(memory, "blk", axis=2, tiled=True)
    mem_proj = product(whole_memory.reshape(local_seqs * mem_count, model_width), cross_kv)
    cross_keys = mem_proj[:, :model_width].astype(HALF_TYPE)
    cross_values = (mem_proj[:, model_width:] + proj_bias[4]).astype(HALF_TYPE)
    cq_heads = to_heads(cross_queries.reshape(local_seqs, local_rows, model_width))
    ck_heads = to_heads(cross_keys.reshape(local_seqs, mem_count, model_width))
    cv_heads = to_heads(cross_values.reshape(local_seqs, mem_count, model_width))
    cross_result, cross_max, cross_sum = run_heads(
        partial(head_forward, None), (cq_heads, ck_heads, cv_heads)
    )
    crossed = from_heads(cross_result, local_seqs).reshape(flat_rows, model_width).astype(HALF_TYPE)
    stream_late = stream_mid + product(crossed, cross_out) + proj_bias[5]
    normed_mlp = layer_norm(stream_late, norm_gain[2], norm_bias[2]).astype(HALF_TYPE)
    hidden_pre = product(normed_mlp, fc_in) + fc_in_bias
    hidden_act = jax.nn.gelu(hidden_pre, approximate=False).astype(HALF_TYPE)
    stream_out = stream_late + product(hidden_act, fc_out) + proj_bias[6]
    result = (stream_out * row_mask).reshape(local_seqs, local_rows, model_width).astype(HALF_TYPE)
    grad_late = cotangent.astype(jnp.float32).reshape(flat_rows, model_width) * row_mask
    grad_mlp = grad_late.astype(HALF_TYPE)
    grad_fc_out = product(hidden_act.T, grad_mlp)
    grad_act = product(grad_mlp, fc_out.T)
    gelu_pull = jax.vjp(partial(jax.nn.gelu, approximate=False), hidden_pre)[1]
    grad_pre = gelu_pull(grad_act)[0].astype(HALF_TYPE)
    grad_fc_in = product(normed_mlp.T, grad_pre)
    grad_fc_bias = col_sums(grad_pre)
    norm_pull = jax.vjp(layer_norm, stream_late, norm_gain[2], norm_bias[2])[1]
    grad_x2, gain_two, shift_two = norm_pull(product(grad_pre, fc_in.T))
    grad_two = grad_late + grad_x2
    grad_cross = grad_two.astype(HALF_TYPE)
    grad_cross_out = product(crossed.T, grad_cross)
    grad_crossed = product(grad_cross, cross_out.T).astype(HALF_TYPE)
    cd_heads = to_heads(grad_crossed.reshape(local_seqs, local_rows, model_width))
    cq_grad, ck_grad, cv_grad = run_heads(
        partial(head_backward, None), (cq_heads, ck_heads, cv_heads, cd_heads, cross_max, cross_sum)
    )
    grad_cq = from_heads(cq_grad, local_seqs).reshape(flat_rows, model_width).astype(HALF_TYPE)
    partial_kv = jnp.concatenate(
        [from_heads(ck_grad, local_seqs), from_heads(cv_grad, local_seqs)], axis=2
    )
    grad_ckv = (
        lax.psum(partial_kv, "blk")
        .astype(HALF_TYPE)
        .reshape(local_seqs * mem_count, 2 * model_width)
    )
    grad_memory = product(grad_ckv, own_rows.T).reshape(local_seqs, mem_count, shard_width)
    grad_cross_kv = product(mem_share.T, grad_ckv)
    column_own = (jnp.arange(model_width, dtype=jnp.int32) // shard_width == block_index).astype(
        jnp.float32
    )
    bias_cross_v = col_sums(grad_ckv[:, model_width:]) * column_own
    grad_cross_q = product(normed_cross.T, grad_cq)
    norm_pull = jax.vjp(layer_norm, stream_mid, norm_gain[1], norm_bias[1])[1]
    grad_x1, gain_one, shift_one = norm_pull(product(grad_cq, cross_q.T))
    grad_one = grad_two + grad_x1
    grad_self = grad_one.astype(HALF_TYPE)
    grad_self_out = product(attended.T, grad_self)
    grad_attended = product(grad_self, self_out.T).astype(HALF_TYPE)
    sd_heads = to_heads(grad_attended.reshape(local_seqs, local_rows, model_width))
    sq_grad, sk_grad, sv_grad = run_heads(
        partial(head_backward, offset),
        (query_heads, key_heads, value_heads, sd_heads, self_max, self_sum),
    )
    key_part, value_part = (
        lax.psum_scatter(from_heads(sk_grad, local_seqs), "blk", scatter_dimension=1, tiled=True),
        lax.psum_scatter(from_heads(sv_grad, local_seqs), "blk", scatter_dimension=1, tiled=True),
    )
    grad_q = from_heads(sq_grad, local_seqs).reshape(flat_rows, model_width).astype(HALF_TYPE)
    grad_k = key_part.astype(HALF_TYPE).reshape(flat_rows, model_width)
    grad_v = value_part.astype(HALF_TYPE).reshape(flat_rows, model_width)
    grad_qkv = jnp.concatenate([grad_q, grad_k, grad_v], axis=1)
    grad_self_qkv = product(normed_self.T, grad_qkv)
    norm_pull = jax.vjp(layer_norm, stream_in, norm_gain[0], norm_bias[0])[1]
    grad_x0, gain_zero, shift_zero = norm_pull(product(grad_qkv, self_qkv.T))
    grad_tokens = (grad_one + grad_x0).reshape(local_seqs, local_rows, model_width)
    gain_terms = jnp.stack([gain_zero, gain_one, gain_two])
    shift_terms = jnp.stack([shift_zero, shift_one, shift_two])
    bias_terms = jnp.stack(
        [
            col_sums(grad_q),
            col_sums(grad_v),
            col_sums(grad_self),
            col_sums(grad_cq),
            bias_cross_v,
            col_sums(grad_cross),
            col_sums(grad_mlp),
        ]
    )
    shares = (
        lax.psum_scatter(
            gain_terms.astype(jnp.bfloat16), "blk", scatter_dimension=1, tiled=True
        ).astype(jnp.float32),
        lax.psum_scatter(
            shift_terms.astype(jnp.bfloat16), "blk", scatter_dimension=1, tiled=True
        ).astype(jnp.float32),
        lax.psum_scatter(
            grad_self_qkv.astype(jnp.bfloat16), "blk", scatter_dimension=0, tiled=True
        ).astype(jnp.float32),
        lax.psum_scatter(
            grad_self_out.astype(jnp.bfloat16), "blk", scatter_dimension=0, tiled=True
        ).astype(jnp.float32),
        lax.psum_scatter(
            grad_cross_q.astype(jnp.bfloat16), "blk", scatter_dimension=0, tiled=True
        ).astype(jnp.float32),
        lax.psum_scatter(
            grad_cross_out.astype(jnp.bfloat16), "blk", scatter_dimension=0, tiled=True
        ).astype(jnp.float32),
        lax.psum_scatter(
            grad_fc_in.astype(jnp.bfloat16), "blk", scatter_dimension=0, tiled=True
        ).astype(jnp.float32),
        lax.psum_scatter(
            grad_fc_out.astype(jnp.bfloat16), "blk", scatter_dimension=0, tiled=True
        ).astype(jnp.float32),
        lax.psum_scatter(
            grad_fc_bias.astype(jnp.bfloat16), "blk", scatter_dimension=0, tiled=True
        ).astype(jnp.float32),
        lax.psum_scatter(
            bias_terms.astype(jnp.bfloat16), "blk", scatter_dimension=1, tiled=True
        ).astype(jnp.float32),
    )
    totals = (
        lax.psum(shares[0].astype(jnp.bfloat16), "page").astype(jnp.float32),
        lax.psum(shares[1].astype(jnp.bfloat16), "page").astype(jnp.float32),
        lax.psum(shares[2].astype(jnp.bfloat16), "page").astype(jnp.float32),
        lax.psum(shares[3].astype(jnp.bfloat16), "page").astype(jnp.float32),
        lax.psum(shares[4].astype(jnp.bfloat16), "page").astype(jnp.float32),
        lax.psum(shares[5].astype(jnp.bfloat16), "page").astype(jnp.float32),
        lax.psum(shares[6].astype(jnp.bfloat16), "page").astype(jnp.float32),
        lax.psum(shares[7].astype(jnp.bfloat16), "page").astype(jnp.float32),
        lax.psum(shares[8].astype(jnp.bfloat16), "page").astype(jnp.float32),
        lax.psum(shares[9].astype(jnp.bfloat16), "page").astype(jnp.float32),
        lax.psum(grad_cross_kv.astype(jnp.bfloat16), "page").astype(jnp.float32),
    )
    return (
        result,
        grad_tokens,
        grad_memory,
        totals[0],
        totals[1],
        totals[2],
        totals[3],
        totals[4],
        totals[10],
        totals[5],
        totals[6],
        totals[7],
        totals[8],
        totals[9],
    )


def solution(mesh):
    return jax.shard_map(
        shards,
        mesh=mesh,
        in_specs=(
            P("page", "blk", None),
            P("page", None, "blk"),
            P("page"),
            P("page"),
            P(),
            P(),
            P(),
            P(),
            P(),
            P(),
            P(),
            P(),
            P(),
            P(),
            P(),
            P("page", "blk", None),
        ),
        out_specs=(
            P("page", "blk", None),
            P("page", "blk", None),
            P("page", None, "blk"),
            P(None, "blk"),
            P(None, "blk"),
            P("blk", None),
            P("blk", None),
            P("blk", None),
            P("blk", None),
            P("blk", None),
            P("blk", None),
            P("blk", None),
            P("blk"),
            P(None, "blk"),
        ),
        check_vma=False,
    )
```

profile of v0, /device:TPU:0, one launch (start us, length us, event | category | flops | bytes accessed | tf_op | source)
XLA Modules:
  0.0 2953.8 jit_solution(15977713299414228939)
XLA Ops:
  111.7 110.5 %all-gather.3.cloned.1.call-done = bf16[2,4096,2048]{1,2,0:T(8,128)(2,1)} async-done(((bf16[2,512,2048]{1,2,0:T(8,128)(2,1)}), bf16[2,4096,2048]{1,2,0:T(8,128)(2,1)}) %all-gather.3.cloned.1.call-update) | async-done | bytes 33554448 | tf_op jit(solution)/shard_map/all_gather | solution.py:137
  222.3 23.2 fusion.157
  247.1 382.2 %while.56 = (s32[]{:T(128)}, bf16[8,4,512,64]{2,3,1,0:T(8,128)(2,1)}, f32[8,4,512]{2,1,0:T(4,128)S(1)}, f32[8,4,512]{2,1,0:T(4,128)S(1)}, s32[]{:T(128)}, /*inde...) while((s32[]{:T(128)}, ...), condition=%wide.region_5.6_spmd, body=%wide.region_2.5_spmd.sunk | while | flops 2250240512 | bytes 114112624 | solution.py:52
  279.3 15.7 fusion.235
  327.0 15.7 fusion.235
  517.8 15.7 fusion.235
  565.5 15.7 fusion.235
  655.8 43.9 %while.57 = (s32[]{:T(128)}, bf16[8,4,512,64]{2,3,1,0:T(8,128)(2,1)}, f32[8,4,512]{2,1,0:T(4,128)S(1)}, f32[8,4,512]{2,1,0:T(4,128)S(1)}, bf16[8,4,512,64]{2,3,1...) while((s32[]{:T(128)}, ...), condition=%wide.region_11.12_spmd, body=%wide.region_8.11_spmd.sunk | while | flops 319115264 | bytes 15968353 | solution.py:52
  720.2 55.5 %fusion.153 = (bf16[4096]{0:T(1024)(128)(2,1)}, bf16[1024,4096]{1,0:T(8,128)(2,1)}, f32[1024,4096]{1,0:T(8,128)}) fusion(f32[1024,4096]{1,0:T(8,128)S(1)} %fusion.148, f32[4096]{0:T(1024)S(1)} %copy-done.64, bf16[1024,1024]{1,0:T(8,128)(2,1)} %fusion.127, bf16[4096,1024]{1,0:T(8,128)(2,1)} %param.36), kind=kOutput, calls=%fused_computation.240 | convolution fusion | flops 8900308992 | bytes 52453376 | tf_op jit(solution)/shard_map/dot_general | solution.py:24
  775.7 16.0 multiply_reduce_fusion.3
  814.5 112.4 %while.58 = (s32[]{:T(128)}, bf16[8,4,512,64]{2,3,1,0:T(8,128)(2,1)}, f32[8,4,588,64]{2,3,1,0:T(8,128)}, f32[8,4,588,64]{2,3,1,0:T(8,128)}, bf16[8,4,512,64]{2,3...) while((s32[]{:T(128)}, ...), condition=%wide.region_18.19_spmd, body=%wide.region_16.18_spmd.sunk | while | flops 781820928 | bytes 40064120 | solution.py:52
  957.0 889.3 %while.59 = (s32[]{:T(128)}, bf16[8,4,512,64]{2,3,1,0:T(8,128)(2,1)}, f32[8,4,4096,64]{2,3,1,0:T(8,128)}, f32[8,4,4096,64]{2,3,1,0:T(8,128)}, s32[]{:T(128)}, /*...) while((s32[]{:T(128)}, ...), condition=%wide.region_23.24_spmd, body=%wide.region_21.23_spmd.sunk | while | flops 5455870464 | bytes 272180352 | solution.py:52
  959.8 17.3 fusion.259
  977.1 27.1 multiply_reduce_fusion.14
  1004.2 27.8 multiply_convert_fusion.8
  1032.0 15.7 fusion.262
  1070.9 17.3 fusion.259
  1088.2 27.1 multiply_reduce_fusion.14
  1115.4 27.8 multiply_convert_fusion.8
  1182.1 17.3 fusion.259
  1199.3 27.1 multiply_reduce_fusion.14
  1226.5 27.8 multiply_convert_fusion.8
  1293.1 17.3 fusion.259
  1310.4 27.1 multiply_reduce_fusion.14
  1337.6 27.8 multiply_convert_fusion.8
  1404.1 17.3 fusion.259
  1421.4 27.1 multiply_reduce_fusion.14
  1448.6 27.8 multiply_convert_fusion.8
  1476.3 15.7 fusion.262
  1515.3 17.3 fusion.259
  1532.5 27.1 multiply_reduce_fusion.14
  1559.7 27.8 multiply_convert_fusion.8
  1587.5 15.7 fusion.262
  1626.4 17.3 fusion.259
  1643.7 27.2 multiply_reduce_fusion.14
  1670.9 27.8 multiply_convert_fusion.8
  1737.5 17.3 fusion.259
  1754.8 27.1 multiply_reduce_fusion.14
  1781.9 27.8 multiply_convert_fusion.8
  1868.4 18.4 multiply_convert_fusion.2
  1903.3 16.2 convolution_convert_fusion.1
  1925.2 126.5 %reduce-scatter.18.cloned.1.call-done = f32[2,512,1024]{1,2,0:T(8,128)} async-done(((f32[2,4096,1024]{1,2,0:T(8,128)}), f32[2,512,1024]{1,2,0:T(8,128)}) %reduce-scatter.18.cloned.1.call-update) | async-done | bytes 4194320 | tf_op jit(solution)/shard_map/reduce_scatter | solution.py:213
  2060.9 200.0 %reduce-scatter.20.cloned.1.call-done = f32[2,512,1024]{1,2,0:T(8,128)} async-done(((f32[2,4096,1024]{1,2,0:T(8,128)}), f32[2,512,1024]{1,2,0:T(8,128)}) %reduce-scatter.20.cloned.1.call-update) | async-done | bytes 4194320 | tf_op jit(solution)/shard_map/reduce_scatter | solution.py:214
  2305.6 244.0 %all-reduce.7 = bf16[2,588,2048]{2,1,0:T(8,128)(2,1)} all-reduce(f32[2,588,2048]{2,1,0:T(8,128)} %pad_maximum_fusion), channel_id=1, replica_groups=mesh['page'=4,'blk'=8] {'blk'}, use_global_device_ids=true, to_apply=%region_28.29 | all-reduce | flops 2408448 | bytes 14450688 | tf_op jit(solution)/shard_map/psum | solution.py:190
  2595.5 65.4 %reduce-scatter.22.cloned.1.call-done = bf16[128,3072]{1,0:T(8,128)(2,1)} async-done(((bf16[1024,3072]{1,0:T(8,128)(2,1)}), bf16[128,3072]{1,0:T(8,128)(2,1)}) %reduce-scatter.22.cloned.1.call-update) | async-done | bytes 786448 | tf_op jit(solution)/shard_map/reduce_scatter | solution.py:244
  2699.7 35.8 %reduce-scatter.36.cloned.1.call-done = bf16[128,3]{1,0:T(8,128)(2,1)} async-done(((bf16[1024,3]{1,0:T(8,128)(2,1)}), bf16[128,3]{1,0:T(8,128)(2,1)}) %reduce-scatter.36.cloned.1.call-update) | async-done | bytes 784
  2736.3 36.4 %reduce-scatter.38.cloned.1.call-done = bf16[128,7]{1,0:T(8,128)(2,1)} async-done(((bf16[1024,7]{1,0:T(8,128)(2,1)}), bf16[128,7]{1,0:T(8,128)(2,1)}) %reduce-scatter.38.cloned.1.call-update) | async-done | bytes 1808
  2787.9 145.7 %all-reduce.6.cloned.1.call-done = (bf16[128,2048]{0,1:T(8,128)(2,1)}, bf16[128,3072]{1,0:T(8,128)(2,1)}, bf16[128,1024]{1,0:T(8,128)(2,1)}, bf16[128,1024]{1,0:...) async-done(((bf16[128,2048]{0,1:T(8,128)(2,1)}, bf16[128,3072]{1,0:T(8,128)(2,1)}, bf16[128,1024]{1,0:T(8,128)(2,1)}, ...) | async-done | bytes 4194320 | tf_op jit(solution)/shard_map/psum | solution.py:280
  (573 shorter events, 1154.6 us)
Async XLA Ops:
  7.2 631.5 %copy-start = (bf16[1024,1024]{1,0:T(8,128)(2,1)S(1)}, bf16[1024,1024]{1,0:T(8,128)(2,1)}, u32[]{:S(2)}) copy-start(bf16[1024,1024]{1,0:T(8,128)(2,1)} %param.32) | copy-start | bytes 6291460
  7.2 6.6 copy-start.80
  7.2 47.9 %all-gather.5.cloned.1.call-start = ((), (), s32[]{:S(2)}) async-start(), calls=%async_computation.12 | async-start | bytes 2709504 | tf_op jit(solution)/shard_map/all_gather | solution.py:150
  8.0 214.3 %all-gather.3.cloned.1.call-start = ((), (), s32[]{:S(2)}) async-start(), calls=%async_computation.11 | async-start | bytes 37748736 | tf_op jit(solution)/shard_map/all_gather | solution.py:137
  8.0 7.3 copy-start.96
  15.3 6.7 copy-start.25
  40.0 2011.7 %reduce-scatter.18.cloned.1.call-start = ((), (), s32[]{:S(2)}) async-start(), calls=%async_computation.13 | async-start | bytes 37748736 | tf_op jit(solution)/shard_map/reduce_scatter | solution.py:213
  41.4 12.0 copy-start.48
  707.0 13.1 copy-start.13
  707.1 13.1 copy-start.56
  707.7 12.5 copy-start.70
  708.2 12.0 copy-start.64
  720.2 55.5 %copy-start.12 = (f32[1024,4096]{1,0:T(8,128)}, f32[1024,4096]{1,0:T(8,128)S(1)}, u32[]{:S(2)}) copy-start(f32[1024,4096]{1,0:T(8,128)S(1)} %fusion.148) | copy-start | bytes 50331652
  720.2 55.5 %copy-start.74 = (f32[1,1024]{1,0:T(1,128)S(1)}, f32[1,1024]{1,0:T(1,128)}, u32[]{:S(2)}) copy-start(f32[1,1024]{1,0:T(1,128)} %get-tuple-element.425) | copy-start | bytes 12292
  775.7 16.1 copy-start.62
  775.7 16.1 copy-start.14
  775.7 16.1 copy-start.57
  775.7 16.1 copy-start.71
  1846.3 414.6 %reduce-scatter.20.cloned.1.call-start = ((), (), s32[]{:S(2)}) async-start(), calls=%async_computation.14 | async-start | bytes 37748736 | tf_op jit(solution)/shard_map/reduce_scatter | solution.py:214
  1846.9 739.1 %reduce-scatter.28.cloned.1.call-start = ((), (), s32[]{:S(2)}) async-start(), calls=%async_computation.18 | async-start | bytes 2359296 | tf_op jit(solution)/shard_map/reduce_scatter | solution.py:253
  1853.2 8.5 copy-start.28
  1853.2 732.8 %reduce-scatter.26.cloned.1.call-start = ((), (), s32[]{:S(2)}) async-start(), calls=%async_computation.17 | async-start | bytes 2359296 | tf_op jit(solution)/shard_map/reduce_scatter | solution.py:250
  1861.7 6.7 copy-start.65
  1861.7 724.3 %reduce-scatter.24.cloned.1.call-start = ((), (), s32[]{:S(2)}) async-start(), calls=%async_computation.16 | async-start | bytes 2359296 | tf_op jit(solution)/shard_map/reduce_scatter | solution.py:247
  1868.3 717.7 %reduce-scatter.32.cloned.1.call-start = ((), (), s32[]{:S(2)}) async-start(), calls=%async_computation.20 | async-start | bytes 9437184 | tf_op jit(solution)/shard_map/reduce_scatter | solution.py:259
  1868.4 22.9 copy-start.24
  1902.6 692.9 %reduce-scatter.30.cloned.1.call-start = ((), (), s32[]{:S(2)}) async-start(), calls=%async_computation.19 | async-start | bytes 9437184 | tf_op jit(solution)/shard_map/reduce_scatter | solution.py:256
  1919.5 741.4 %reduce-scatter.22.cloned.1.call-start = ((), (), s32[]{:S(2)}) async-start(), calls=%async_computation.15 | async-start | bytes 7077888 | tf_op jit(solution)/shard_map/reduce_scatter | solution.py:244
  2282.4 416.5 %reduce-scatter.34.cloned.1.call-start = ((), (), s32[]{:S(2)}) async-start(), calls=%async_computation.21 | async-start | bytes 294912
  2555.2 7.1 copy-start.4
  2555.2 7.1 copy-start.32
  2555.2 7.1 copy-start.33
  2555.2 7.1 copy-start.43
  2555.2 7.1 copy-start.47
  2562.3 11.3 copy-start.52
  2562.3 13.2 copy-start.45
  2573.5 6.6 copy-start.81
  2573.5 7.7 copy-start.37
  2578.7 156.8 %reduce-scatter.36.cloned.1.call-start = ((), (), s32[]{:S(2)}) async-start(), calls=%async_computation.22 | async-start | bytes 294912
  2579.9 192.8 %reduce-scatter.38.cloned.1.call-start = ((), (), s32[]{:S(2)}) async-start(), calls=%async_computation.23 | async-start | bytes 294912
  2581.1 79.8 %copy-start.103 = (u32[32]{0:T(128)S(1)}, u32[32]{0:T(128)}, u32[]{:S(2)}) copy-start(u32[32]{0:T(128)} %constant.215) | copy-start | bytes 388
  2581.2 352.5 %all-reduce.6.cloned.1.call-start = ((), (), s32[]{:S(2)}) async-start(), calls=%async_computation.24 | async-start | bytes 8388608 | tf_op jit(solution)/shard_map/psum | solution.py:280
  2660.9 19.4 copy-start.50
  2661.0 19.4 copy-start.84
  2680.4 15.5 copy-start.19
  2680.4 15.5 copy-start.21
  2933.6 10.4 copy-start.36
  2935.9 9.6 copy-start.35
  (70 other events, 224.0 us)
Sparse Core Ops, SparseCore 0:
  9.9 42.4 all-gather.4
  54.8 167.4 all-gather.2
  1846.4 205.2 reduce-scatter.17
  2055.6 205.2 reduce-scatter.19
  2264.0 41.1 reduce-scatter.27
  2308.7 49.8 reduce-scatter.25
  2361.9 49.9 reduce-scatter.23
  2415.7 104.9 reduce-scatter.31
  2524.2 71.2 reduce-scatter.29
  2599.2 61.7 reduce-scatter.21
  2664.5 33.5 reduce-scatter.33
  2701.9 33.5 reduce-scatter.35
  2739.1 33.5 reduce-scatter.37
  2776.3 157.2 all-reduce.5
where the time goes:
time: 2970 us; the launch traced here: 2950 us
  matrix products  1240 us (42%)
  waiting for transfers between devices  731 us (25%)
  other arithmetic  474 us (16%)
  blocking collectives  269 us (9%)
  local copies, waits for them, and re-layouts  217 us (7%)
    dot_general x32, matrix products, raw_scores(): jnp.einsum('gqd,gkd->gqk', queries, key_rows, preferred_element_type=jnp....  376 us
    psum x1, blocking collectives, shards(): lax.psum(partial_kv, 'blk').astype(HALF_TYPE)  244 us
    convert_element_type x16, other arithmetic, head_backward(): grad_scores = (attn_probs * (grad_probs - row_delta)).astype(HALF_TYPE)  232 us
    dot_general x21, matrix products, product(): return jnp.dot(left_op, right_op, preferred_element_type=jnp.float32)  215 us
    reduce_scatter x1, waiting for transfers between devices, shards(): lax.psum_scatter(from_heads(sv_grad, local_seqs), 'blk', scatter_dimensio...  200 us
    dot_general x16, matrix products, head_backward(): jnp.einsum('gqd,gkd->gqk', grad_out, values, preferred_element_type=jnp.f...  153 us
    dot_general x16, matrix products, head_forward(): jnp.einsum('gqk,gkd->gqd', attn_probs, values, preferred_element_type=jnp...  147 us
    dot_general x16, matrix products, head_backward(): jnp.einsum('gqk,gqd->gkd', attn_probs.astype(HALF_TYPE), grad_out, prefer...  146 us
  transfers between devices with their start and end apart: 14, of which 8 were waited for; matrix products, arithmetic and copies ran while one was open for 10% of the time, Pallas kernels for 0%

commit v1 on v0

v1 whole, which is shorter than its diff:
```python
from functools import partial

import jax
import jax.numpy as jnp
from jax import lax
from jax.experimental import pallas as pl
from jax.experimental.pallas import tpu as pltpu
from jax.sharding import PartitionSpec as P

HEADS = 16
EPSILON = 1e-05
NEG_LARGE = -1e30
HALF = jnp.bfloat16
F32 = jnp.float32
LOG2E = 1.4426950408889634
LN2 = 0.6931471805599453
NT = (((1,), (1,)), ((), ()))
NN = (((1,), (0,)), ((), ()))
TN = (((0,), (0,)), ((), ()))
VMEM_LIMIT = 56 * 2**20


def mxu(left_op, right_op, dims=NN):
    return lax.dot_general(left_op, right_op, dims, preferred_element_type=F32)


def head_lanes(width, head, head_dim):
    lane = lax.broadcasted_iota(jnp.int32, (1, width), 1)
    return (lane >= head * head_dim) & (lane < (head + 1) * head_dim)


def one_head(tensor, head, n_heads, head_dim):
    if n_heads == 1:
        return tensor
    return jnp.where(
        head_lanes(tensor.shape[-1], head, head_dim), tensor, jnp.zeros_like(tensor)
    )


def causal(scores, key_start, query_start):
    key_pos = key_start + lax.broadcasted_iota(jnp.int32, scores.shape, 0)
    query_pos = query_start + lax.broadcasted_iota(jnp.int32, scores.shape, 1)
    return jnp.where(key_pos <= query_pos, scores, NEG_LARGE)


def load_pieces(scalars, pieces, whole, sem):
    rows = pieces[0].shape[0]
    me = scalars[1]
    copies = []
    for step, piece in enumerate(pieces):
        start = pl.multiple_of(lax.bitwise_xor(me, step) * rows, rows)
        copies.append(pltpu.make_async_copy(piece, whole.at[pl.ds(start, rows)], sem.at[step]))
    for copy in copies:
        copy.start()
    return copies


def store_pieces(scalars, pieces, whole, sem):
    rows = pieces[0].shape[0]
    me = scalars[1]
    copies = []
    for step, piece in enumerate(pieces):
        start = pl.multiple_of(lax.bitwise_xor(me, step) * rows, rows)
        copies.append(pltpu.make_async_copy(whole.at[pl.ds(start, rows)], piece, sem.at[step]))
    for copy in copies:
        copy.start()
    for copy in copies:
        copy.wait()


def self_forward_kernel(scalars, *refs, n, n_heads, head_dim, q_block, k_block, stat_block):
    pieces, refs = refs[:n], refs[n:]
    out_pieces, refs = refs[:n], refs[n:]
    kept_out, log_sums, whole, values_t, sem = refs
    width = n_heads * head_dim
    index = pl.program_id(0)
    k_blocks = values_t.shape[0]

    @pl.when(index == 0)
    def _():
        for copy in load_pieces(scalars, pieces, whole, sem):
            copy.wait()
        for b in range(k_blocks):
            values_t[b] = whole[b * k_block : (b + 1) * k_block, 2 * width :].T

    start = pl.multiple_of(index * q_block, q_block)
    q_rows = pl.ds(start, q_block)
    live = start < scalars[0]

    @pl.when(jnp.logical_not(live))
    def _():
        kept_out[q_rows, :] = jnp.zeros((q_block, width), HALF)
        log_sums[...] = jnp.zeros_like(log_sums)

    @pl.when(live)
    def _():
        query = whole[q_rows, :width]
        queries = [one_head(query, h, n_heads, head_dim) for h in range(n_heads)]

        def step(kb, carry, masked):
            keys = whole[pl.ds(pl.multiple_of(kb * k_block, k_block), k_block), width : 2 * width]
            value_t = values_t[kb]
            out = []
            for h in range(n_heads):
                top, total, acc = carry[h]
                scores = mxu(keys, queries[h], NT)
                if masked:
                    scores = causal(scores, kb * k_block, start)
                new_top = jnp.maximum(top, jnp.max(scores, axis=0, keepdims=True))
                probs = jnp.exp2(scores - new_top)
                scale = jnp.exp2(top - new_top)
                total = total * scale + jnp.sum(probs, axis=0, keepdims=True)
                part = mxu(value_t[h * head_dim : (h + 1) * head_dim], probs.astype(HALF))
                out.append((new_top, total, acc * scale + part))
            return tuple(out)

        carry = tuple(
            (
                jnp.full((1, q_block), NEG_LARGE, F32),
                jnp.zeros((1, q_block), F32),
                jnp.zeros((head_dim, q_block), F32),
            )
            for _ in range(n_heads)
        )
        ratio = q_block // k_block
        carry = lax.fori_loop(0, index * ratio, lambda kb, c: step(kb, c, False), carry)
        for t in range(ratio):
            carry = step(index * ratio + t, carry, True)
        result_t = jnp.concatenate([acc / total for _, total, acc in carry], axis=0)
        kept_out[q_rows, :] = result_t.T.astype(HALF)
        for h, (top, total, _) in enumerate(carry):
            log_sum = top + jnp.log2(total)
            for t in range(q_block // stat_block):
                log_sums[t, h : h + 1, :] = log_sum[:, t * stat_block : (t + 1) * stat_block]

    @pl.when(index == pl.num_programs(0) - 1)
    def _():
        store_pieces(scalars, out_pieces, kept_out, sem)


def self_forward(scalars, pieces, n_heads, head_dim):
    n, rows = len(pieces), pieces[0].shape[0]
    length, width = n * rows, n_heads * head_dim
    q_block, k_block, stat_block = 1024, 512, 512
    any_spec = pl.BlockSpec(memory_space=pl.ANY)
    result = pl.pallas_call(
        partial(
            self_forward_kernel,
            n=n,
            n_heads=n_heads,
            head_dim=head_dim,
            q_block=q_block,
            k_block=k_block,
            stat_block=stat_block,
        ),
        grid_spec=pltpu.PrefetchScalarGridSpec(
            num_scalar_prefetch=1,
            grid=(length // q_block,),
            in_specs=[any_spec] * n,
            out_specs=[any_spec] * n
            + [
                pl.BlockSpec((length, width), lambda i, s: (0, 0)),
                pl.BlockSpec((q_block // stat_block, n_heads, stat_block), lambda i, s: (i, 0, 0)),
            ],
            scratch_shapes=[
                pltpu.VMEM((length, 3 * width), HALF),
                pltpu.VMEM((length // k_block, width, k_block), HALF),
                pltpu.SemaphoreType.DMA((n,)),
            ],
        ),
        out_shape=[jax.ShapeDtypeStruct((rows, width), HALF)] * n
        + [
            jax.ShapeDtypeStruct((length, width), HALF),
            jax.ShapeDtypeStruct((length // stat_block, n_heads, stat_block), F32),
        ],
        compiler_params=pltpu.CompilerParams(vmem_limit_bytes=VMEM_LIMIT),
        cost_estimate=pl.CostEstimate(
            flops=2 * 2 * length * length * width,
            bytes_accessed=length * width * 10,
            transcendentals=n_heads * length * length // 2,
        ),
        name="self_forward",
    )(scalars, *pieces)
    return result[:n], result[n], result[n + 1]


def self_backward_kernel(scalars, *refs, n, n_heads, head_dim, block):
    pieces, refs = refs[:n], refs[n:]
    grad_pieces, refs = refs[:n], refs[n:]
    kept_out, log_sums, refs = refs[0], refs[1], refs[2:]
    out_pieces, refs = refs[:n], refs[n:]
    whole, grads, query_heads, grad_heads, deltas, query_sums, result, sem, grad_sem = refs
    width = n_heads * head_dim
    index = pl.program_id(0)
    blocks = query_heads.shape[1]
    span = scalars[0]

    @pl.when(index == 0)
    def _():
        copies = load_pieces(scalars, pieces, whole, sem)
        copies += load_pieces(scalars, grad_pieces, grads, grad_sem)
        query_sums[...] = jnp.zeros_like(query_sums)
        for copy in copies:
            copy.wait()
        for b in range(blocks):
            rows = slice(b * block, (b + 1) * block)
            query, grad = whole[rows, :width], grads[rows, :]
            products = (grad.astype(F32) * kept_out[rows, :].astype(F32)).T
            for h in range(n_heads):
                deltas[b, h : h + 1, :] = jnp.sum(
                    products[h * head_dim : (h + 1) * head_dim], axis=0, keepdims=True
                )
                query_heads[h, b] = one_head(query, h, n_heads, head_dim)
                grad_heads[h, b] = one_head(grad, h, n_heads, head_dim)

    start = pl.multiple_of(index * block, block)
    k_rows = pl.ds(start, block)
    live = start < span

    @pl.when(jnp.logical_not(live))
    def _():
        result[k_rows, width:] = jnp.zeros((block, 2 * width), HALF)

    @pl.when(live)
    def _():
        keys = whole[k_rows, width : 2 * width]
        values = whole[k_rows, 2 * width :]
        keys_t = keys.T

        def step(qb, carry, masked):
            grad_keys, grad_values = carry
            for h in range(n_heads):
                query, grad = query_heads[h, qb], grad_heads[h, qb]
                scores = mxu(keys, query, NT)
                if masked:
                    scores = causal(scores, start, qb * block)
                probs = jnp.exp2(scores - log_sums[qb, h : h + 1, :])
                grad_probs = mxu(values, grad, NT)
                grad_scores = (probs * (grad_probs - deltas[qb, h : h + 1, :])).astype(HALF)
                grad_values = grad_values + mxu(probs.astype(HALF), grad)
                grad_keys = grad_keys + mxu(grad_scores, query)
                lanes = slice(h * head_dim, (h + 1) * head_dim)
                query_sums[qb, lanes, :] += mxu(keys_t[lanes], grad_scores)
            return grad_keys, grad_values

        zero = jnp.zeros((block, width), F32)
        carry = step(index, (zero, zero), True)
        live_blocks = (span + block - 1) // block
        grad_keys, grad_values = lax.fori_loop(
            index + 1, live_blocks, lambda qb, c: step(qb, c, False), carry
        )
        result[k_rows, width : 2 * width] = (grad_keys * LN2).astype(HALF)
        result[k_rows, 2 * width :] = grad_values.astype(HALF)

    @pl.when(index == pl.num_programs(0) - 1)
    def _():
        for b in range(blocks):
            result[b * block : (b + 1) * block, :width] = (query_sums[b] * 0.125).T.astype(HALF)
        store_pieces(scalars, out_pieces, result, sem)


def self_backward(scalars, pieces, grad_pieces, kept_out, log_sums, n_heads, head_dim):
    n, rows = len(pieces), pieces[0].shape[0]
    length, width = n * rows, n_heads * head_dim
    block = log_sums.shape[2]
    blocks = length // block
    any_spec = pl.BlockSpec(memory_space=pl.ANY)
    return pl.pallas_call(
        partial(self_backward_kernel, n=n, n_heads=n_heads, head_dim=head_dim, block=block),
        grid_spec=pltpu.PrefetchScalarGridSpec(
            num_scalar_prefetch=1,
            grid=(blocks,),
            in_specs=[any_spec] * (2 * n)
            + [
                pl.BlockSpec((length, width), lambda i, s: (0, 0)),
                pl.BlockSpec((blocks, n_heads, block), lambda i, s: (0, 0, 0)),
            ],
            out_specs=[any_spec] * n,
            scratch_shapes=[
                pltpu.VMEM((length, 3 * width), HALF),
                pltpu.VMEM((length, width), HALF),
                pltpu.VMEM((n_heads, blocks, block, width), HALF),
                pltpu.VMEM((n_heads, blocks, block, width), HALF),
                pltpu.VMEM((blocks, n_heads, block), F32),
                pltpu.VMEM((blocks, width, block), F32),
                pltpu.VMEM((length, 3 * width), HALF),
                pltpu.SemaphoreType.DMA((n,)),
                pltpu.SemaphoreType.DMA((n,)),
            ],
        ),
        out_shape=[jax.ShapeDtypeStruct((rows, 3 * width), HALF)] * n,
        compiler_params=pltpu.CompilerParams(vmem_limit_bytes=VMEM_LIMIT),
        cost_estimate=pl.CostEstimate(
            flops=5 * 2 * length * length * width // 2,
            bytes_accessed=length * width * 20,
            transcendentals=n_heads * length * length // 2,
        ),
        name="self_backward",
    )(scalars, *pieces, *grad_pieces, kept_out, log_sums)


def cross_scores(keys, query, mem_count):
    scores = mxu(keys, query, NT)
    padded = scores.shape[0]
    if padded == mem_count:
        return scores
    whole = mem_count // 8 * 8
    tail = scores[whole:]
    position = whole + lax.broadcasted_iota(jnp.int32, tail.shape, 0)
    tail = jnp.where(position < mem_count, tail, NEG_LARGE)
    return jnp.concatenate([scores[:whole], tail], axis=0)


def cross_forward_kernel(scalars, query_ref, key_ref, value_ref, out_ref, log_sums, *, mem_count, head_dim):
    rows, width = query_ref.shape
    live = scalars[1] * rows < scalars[0]

    @pl.when(jnp.logical_not(live))
    def _():
        out_ref[...] = jnp.zeros_like(out_ref)
        log_sums[...] = jnp.zeros_like(log_sums)

    @pl.when(live)
    def _():
        n_heads = width // head_dim
        query, keys = query_ref[...], key_ref[...]
        values_t = value_ref[...].T
        results = []
        for h in range(n_heads):
            scores = cross_scores(keys, one_head(query, h, n_heads, head_dim), mem_count)
            top = jnp.max(scores, axis=0, keepdims=True)
            probs = jnp.exp2(scores - top)
            total = jnp.sum(probs, axis=0, keepdims=True)
            lanes = slice(h * head_dim, (h + 1) * head_dim)
            results.append(mxu(values_t[lanes], probs.astype(HALF)) / total)
            log_sums[0, h : h + 1, :] = top + jnp.log2(total)
        out_ref[...] = jnp.concatenate(results, axis=0).T.astype(HALF)


def cross_forward(scalars, query, keys, values, mem_count, head_dim):
    rows, model_width = query.shape
    padded = keys.shape[0]
    width = 128
    groups, n_heads = model_width // width, width // head_dim
    column = lambda count: pl.BlockSpec((count, width), lambda g, s: (0, g))
    return pl.pallas_call(
        partial(cross_forward_kernel, mem_count=mem_count, head_dim=head_dim),
        grid_spec=pltpu.PrefetchScalarGridSpec(
            num_scalar_prefetch=1,
            grid=(groups,),
            in_specs=[column(rows), column(padded), column(padded)],
            out_specs=[column(rows), pl.BlockSpec((1, n_heads, rows), lambda g, s: (g, 0, 0))],
        ),
        out_shape=[
            jax.ShapeDtypeStruct((rows, model_width), HALF),
            jax.ShapeDtypeStruct((groups, n_heads, rows), F32),
        ],
        compiler_params=pltpu.CompilerParams(vmem_limit_bytes=VMEM_LIMIT),
        cost_estimate=pl.CostEstimate(
            flops=4 * 2 * rows * padded * model_width,
            bytes_accessed=(rows + padded) * model_width * 4,
            transcendentals=rows * padded * model_width // head_dim,
        ),
        name="cross_forward",
    )(scalars, query, keys, values)


def cross_backward_kernel(
    scalars,
    query_ref,
    key_ref,
    value_ref,
    grad_ref,
    out_ref,
    log_sums,
    grad_query,
    grad_key,
    grad_value,
    *,
    mem_count,
    head_dim,
):
    rows, width = query_ref.shape
    padded = key_ref.shape[0]
    live = scalars[1] * rows < scalars[0]

    @pl.when(jnp.logical_not(live))
    def _():
        grad_query[...] = jnp.zeros_like(grad_query)
        grad_key[...] = jnp.zeros_like(grad_key)
        grad_value[...] = jnp.zeros_like(grad_value)

    @pl.when(live)
    def _():
        n_heads = width // head_dim
        query_all, keys, values, grad_all = query_ref[...], key_ref[...], value_ref[...], grad_ref[...]
        keys_t = keys.T
        products = (grad_all.astype(F32) * out_ref[...].astype(F32)).T
        query_parts = []
        key_sum = jnp.zeros((padded, width), F32)
        value_sum = jnp.zeros((padded, width), F32)
        for h in range(n_heads):
            lanes = slice(h * head_dim, (h + 1) * head_dim)
            query = one_head(query_all, h, n_heads, head_dim)
            grad = one_head(grad_all, h, n_heads, head_dim)
            delta = jnp.sum(products[lanes], axis=0, keepdims=True)
            scores = cross_scores(keys, query, mem_count)
            probs = jnp.exp2(scores - log_sums[0, h : h + 1, :])
            grad_probs = mxu(values, grad, NT)
            grad_scores = (probs * (grad_probs - delta)).astype(HALF)
            value_sum = value_sum + mxu(probs.astype(HALF), grad)
            key_sum = key_sum + mxu(grad_scores, query)
            query_parts.append(mxu(keys_t[lanes], grad_scores))
        grad_query[...] = (jnp.concatenate(query_parts, axis=0) * 0.125).T.astype(HALF)
        grad_key[...] = (key_sum * LN2).astype(HALF)
        grad_value[...] = value_sum.astype(HALF)


def cross_backward(scalars, query, keys, values, grad, kept_out, log_sums, mem_count, head_dim):
    rows, model_width = query.shape
    padded = keys.shape[0]
    width = 128
    groups, n_heads = model_width // width, width // head_dim
    column = lambda count: pl.BlockSpec((count, width), lambda g, s: (0, g))
    return pl.pallas_call(
        partial(cross_backward_kernel, mem_count=mem_count, head_dim=head_dim),
        grid_spec=pltpu.PrefetchScalarGridSpec(
            num_scalar_prefetch=1,
            grid=(groups,),
            in_specs=[
                column(rows),
                column(padded),
                column(padded),
                column(rows),
                column(rows),
                pl.BlockSpec((1, n_heads, rows), lambda g, s: (g, 0, 0)),
            ],
            out_specs=[column(rows), column(padded), column(padded)],
        ),
        out_shape=[
            jax.ShapeDtypeStruct((rows, model_width), HALF),
            jax.ShapeDtypeStruct((padded, model_width), HALF),
            jax.ShapeDtypeStruct((padded, model_width), HALF),
        ],
        compiler_params=pltpu.CompilerParams(vmem_limit_bytes=VMEM_LIMIT),
        cost_estimate=pl.CostEstimate(
            flops=10 * 2 * rows * padded * model_width,
            bytes_accessed=(rows + padded) * model_width * 10,
            transcendentals=rows * padded * model_width // head_dim,
        ),
        name="cross_backward",
    )(scalars, query, keys, values, grad, kept_out, log_sums)


def exchange(columns, n, me):
    width = columns.shape[1] // n
    pieces = []
    for step in range(n):
        piece = lax.dynamic_slice_in_dim(columns, lax.bitwise_xor(me, step) * width, width, 1)
        pieces.append(swap(piece, step, n))
    return pieces


def swap(piece, step, n):
    if step == 0:
        return piece
    return lax.ppermute(piece, "blk", [(k, k ^ step) for k in range(n)])


def gather_columns(pieces, n, me):
    rows, width = pieces[0].shape
    whole = jnp.zeros((rows, n * width), pieces[0].dtype)
    for step, piece in enumerate(pieces):
        received = swap(piece, step, n)
        whole = lax.dynamic_update_slice_in_dim(
            whole, received, lax.bitwise_xor(me, step) * width, 1
        )
    return whole


def normalized(vector):
    centre = vector - jnp.mean(vector, axis=-1, keepdims=True)
    spread = jnp.mean(centre * centre, axis=-1, keepdims=True)
    inverse = lax.rsqrt(spread + EPSILON)
    return centre * inverse, inverse


def norm_backward(unit, inverse, gain, grad):
    scaled = grad * gain
    first = jnp.mean(scaled, axis=-1, keepdims=True)
    second = jnp.mean(scaled * unit, axis=-1, keepdims=True)
    grad_in = inverse * (scaled - first - unit * second)
    return grad_in, jnp.sum(grad * unit, axis=0), jnp.sum(grad, axis=0)


def col_sums(tensor):
    return jnp.sum(tensor.astype(F32), axis=0)


def shards(
    tokens,
    memory,
    end_only,
    lengths,
    norm_gain,
    norm_bias,
    self_qkv,
    self_out,
    cross_q,
    cross_kv,
    cross_out,
    fc_in,
    fc_out,
    fc_in_bias,
    proj_bias,
    cotangent,
    *,
    n,
):
    seqs, rows, model_width = tokens.shape
    mem_count, shard_width = memory.shape[1], memory.shape[2]
    head_dim = model_width // HEADS
    n_heads = HEADS // n
    width = n_heads * head_dim
    flat = seqs * rows
    me = lax.axis_index("blk")
    offset = me * rows
    span = jnp.where(end_only == 1, 1, lengths)
    scalars = [jnp.stack([span[s], me]).astype(jnp.int32) for s in range(seqs)]
    positions = offset + jnp.arange(rows, dtype=jnp.int32)
    row_mask = (positions[None, :] < span[:, None]).astype(F32).reshape(flat, 1)
    q_scale = 0.125 * LOG2E

    qkv_weights = (
        self_qkv.reshape(model_width, 3, n, width).transpose(0, 2, 1, 3).reshape(model_width, -1)
    )
    zeros = jnp.zeros((model_width,), F32)
    qkv_bias = jnp.stack([proj_bias[0], zeros, proj_bias[1]])
    qkv_bias = qkv_bias.reshape(3, n, width).transpose(1, 0, 2).reshape(-1)
    qkv_scale = jnp.broadcast_to(jnp.array([q_scale, 1.0, 1.0], F32)[None, :, None], (n, 3, width))
    qkv_scale = qkv_scale.reshape(-1)

    stream_in = tokens.astype(F32).reshape(flat, model_width)
    unit_self, inverse_self = normalized(stream_in)
    normed_self = (unit_self * norm_gain[0] + norm_bias[0]).astype(HALF)
    kept = []
    for s in range(seqs):
        projected = mxu(normed_self[s * rows : (s + 1) * rows], qkv_weights)
        projected = ((projected + qkv_bias) * qkv_scale).astype(HALF)
        kept.append(exchange(projected, n, me))

    whole_memory = lax.all_gather(memory, "blk", axis=2, tiled=True)
    padded = -(-mem_count // 16) * 16
    whole_memory = jnp.pad(whole_memory, ((0, 0), (0, padded - mem_count), (0, 0)))
    mem_proj = mxu(whole_memory.reshape(seqs * padded, model_width), cross_kv)
    cross_keys = mem_proj[:, :model_width].astype(HALF).reshape(seqs, padded, model_width)
    cross_values = (mem_proj[:, model_width:] + proj_bias[4]).astype(HALF)
    cross_values = cross_values.reshape(seqs, padded, model_width)

    self_saved, attended = [], []
    for s in range(seqs):
        out_pieces, kept_out, log_sums = self_forward(scalars[s], kept[s], n_heads, head_dim)
        self_saved.append((kept_out, log_sums))
        attended.append(gather_columns(out_pieces, n, me))

    mids, crosses, cross_saved = [], [], []
    for s in range(seqs):
        mid = stream_in[s * rows : (s + 1) * rows] + mxu(attended[s], self_out) + proj_bias[2]
        unit, _ = normalized(mid)
        normed = (unit * norm_gain[1] + norm_bias[1]).astype(HALF)
        query = ((mxu(normed, cross_q) + proj_bias[3]) * q_scale).astype(HALF)
        crossed, log_sums = cross_forward(
            scalars[s], query, cross_keys[s], cross_values[s], mem_count, head_dim
        )
        mids.append(mid)
        crosses.append(crossed)
        cross_saved.append((query, log_sums))
    attended = jnp.concatenate(attended, axis=0)
    crossed = jnp.concatenate(crosses, axis=0)
    stream_mid = jnp.concatenate(mids, axis=0)

    stream_late = stream_mid + mxu(crossed, cross_out) + proj_bias[5]
    unit_mlp, inverse_mlp = normalized(stream_late)
    normed_mlp = (unit_mlp * norm_gain[2] + norm_bias[2]).astype(HALF)
    hidden_pre = mxu(normed_mlp, fc_in) + fc_in_bias
    gate = 0.5 * (1.0 + lax.erf(hidden_pre * (0.5**0.5)))
    hidden_act = (hidden_pre * gate).astype(HALF)
    slope = (gate + hidden_pre * (jnp.exp(-0.5 * hidden_pre * hidden_pre) * 0.3989422804014327)).astype(HALF)
    stream_out = stream_late + mxu(hidden_act, fc_out) + proj_bias[6]
    result = (stream_out * row_mask).reshape(seqs, rows, model_width).astype(HALF)

    grad_late = cotangent.astype(F32).reshape(flat, model_width) * row_mask
    grad_mlp = grad_late.astype(HALF)
    grad_fc_out = mxu(hidden_act, grad_mlp, TN)
    grad_pre = (slope.astype(F32) * mxu(grad_mlp, fc_out, NT)).astype(HALF)
    grad_fc_in = mxu(normed_mlp, grad_pre, TN)
    grad_fc_bias = col_sums(grad_pre)
    grad_x2, gain_two, shift_two = norm_backward(
        unit_mlp, inverse_mlp, norm_gain[2], mxu(grad_pre, fc_in, NT)
    )
    grad_two = grad_late + grad_x2
    grad_cross = grad_two.astype(HALF)
    grad_cross_out = mxu(crossed, grad_cross, TN)

    cq_grads, ckv_parts, ones, selfs, dq_pieces = [], [], [], [], []
    gain_one, shift_one = 0.0, 0.0
    normed_cross = []
    self_grads = []
    for s in range(seqs):
        part = slice(s * rows, (s + 1) * rows)
        grad_crossed = mxu(grad_cross[part], cross_out, NT).astype(HALF)
        query, log_sums = cross_saved[s]
        grad_cq, grad_ck, grad_cv = cross_backward(
            scalars[s],
            query,
            cross_keys[s],
            cross_values[s],
            grad_crossed,
            crosses[s],
            log_sums,
            mem_count,
            head_dim,
        )
        cq_grads.append(grad_cq)
        ckv_parts.append(jnp.concatenate([grad_ck, grad_cv], axis=1))
        unit, inverse = normalized(mids[s])
        normed_cross.append((unit * norm_gain[1] + norm_bias[1]).astype(HALF))
        grad_x1, gain, shift = norm_backward(unit, inverse, norm_gain[1], mxu(grad_cq, cross_q, NT))
        gain_one, shift_one = gain_one + gain, shift_one + shift
        grad_one = grad_two[part] + grad_x1
        ones.append(grad_one)
        grad_self = grad_one.astype(HALF)
        selfs.append(grad_self)
        grad_attended = mxu(grad_self, self_out, NT).astype(HALF)
        self_grads.append(exchange(grad_attended, n, me))
    qkv_grads = []
    for s in range(seqs):
        kept_out, log_sums = self_saved[s]
        pieces = self_backward(
            scalars[s], kept[s], self_grads[s], kept_out, log_sums, n_heads, head_dim
        )
        qkv_grads.append(gather_columns(pieces, n, me))

    grad_ckv = lax.psum(jnp.stack(ckv_parts), "blk").reshape(seqs * padded, 2 * model_width)
    own_rows = lax.dynamic_slice_in_dim(cross_kv, me * shard_width, shard_width, 0)
    grad_memory = mxu(grad_ckv, own_rows, NT).reshape(seqs, padded, shard_width)[:, :mem_count]
    own_memory = jnp.pad(memory, ((0, 0), (0, padded - mem_count), (0, 0)))
    grad_cross_kv = mxu(own_memory.reshape(seqs * padded, shard_width), grad_ckv, TN)
    column_own = (jnp.arange(model_width, dtype=jnp.int32) // shard_width == me).astype(F32)
    bias_cross_v = col_sums(grad_ckv[:, model_width:]) * column_own

    grad_cq = jnp.concatenate(cq_grads, axis=0)
    grad_cross_q = mxu(jnp.concatenate(normed_cross, axis=0), grad_cq, TN)
    grad_self = jnp.concatenate(selfs, axis=0)
    grad_self_out = mxu(attended, grad_self, TN)
    grad_qkv = jnp.concatenate(qkv_grads, axis=0)
    grad_self_qkv = mxu(normed_self, grad_qkv, TN)
    grad_x0, gain_zero, shift_zero = norm_backward(
        unit_self, inverse_self, norm_gain[0], mxu(grad_qkv, qkv_weights, NT)
    )
    grad_tokens = (jnp.concatenate(ones, axis=0) + grad_x0).reshape(seqs, rows, model_width)
    qkv_sums = col_sums(grad_qkv).reshape(n, 3, width)
    gain_terms = jnp.stack([gain_zero, gain_one, gain_two])
    shift_terms = jnp.stack([shift_zero, shift_one, shift_two])
    bias_terms = jnp.stack(
        [
            qkv_sums[:, 0].reshape(-1),
            qkv_sums[:, 2].reshape(-1),
            col_sums(grad_self),
            col_sums(grad_cq),
            bias_cross_v,
            col_sums(grad_cross),
            col_sums(grad_mlp),
        ]
    )

    def scatter(tensor, axis):
        return lax.psum_scatter(tensor.astype(HALF), "blk", scatter_dimension=axis, tiled=True)

    def over_pages(tensor):
        return lax.psum(tensor.astype(HALF), "page").astype(F32)

    small = jnp.concatenate(
        [gain_terms, shift_terms, bias_terms, grad_fc_bias.reshape(n, 4, -1).transpose(1, 0, 2).reshape(4, -1)],
        axis=0,
    )
    small = over_pages(scatter(small, 1))
    total_qkv = over_pages(scatter(grad_self_qkv, 0))
    total_qkv = total_qkv.reshape(-1, n, 3, width).transpose(0, 2, 1, 3).reshape(-1, 3 * model_width)
    return (
        result,
        grad_tokens,
        grad_memory,
        small[0:3],
        small[3:6],
        total_qkv,
        over_pages(scatter(grad_self_out, 0)),
        over_pages(scatter(grad_cross_q, 0)),
        over_pages(grad_cross_kv),
        over_pages(scatter(grad_cross_out, 0)),
        over_pages(scatter(grad_fc_in, 0)),
        over_pages(scatter(grad_fc_out, 0)),
        small[13:17].reshape(-1),
        small[6:13],
    )


def solution(mesh):
    rows_spec = P("page", "blk", None)
    return jax.shard_map(
        partial(shards, n=mesh.shape["blk"]),
        mesh=mesh,
        in_specs=(rows_spec, P("page", None, "blk"), P("page"), P("page"))
        + (P(),) * 11
        + (rows_spec,),
        out_specs=(
            rows_spec,
            rows_spec,
            P("page", None, "blk"),
            P(None, "blk"),
            P(None, "blk"),
            P("blk", None),
            P("blk", None),
            P("blk", None),
            P("blk", None),
            P("blk", None),
            P("blk", None),
            P("blk", None),
            P("blk"),
            P(None, "blk"),
        ),
        check_vma=False,
    )
```

time: 2970 us -> 1120 us (0.38)
  matrix products: 1240 us -> 190 us
  other arithmetic: 474 us -> 50 us
  blocking collectives: 269 us -> 12 us
  Pallas kernels: 0 us -> 182 us
  waiting for transfers between devices: 731 us -> 554 us
  local copies, waits for them, and re-layouts: 217 us -> 57.3 us
  starting transfers between devices: 0.96 us -> 60.1 us
    dot_general x133 -> x27, matrix products: 1240 us -> 190 us  [mxu(): return lax.dot_general(left_op, right_op, dims, preferred_element_type=F32)]
    convert_element_type x32 -> x13, other arithmetic: 274 us -> 20.4 us  [the longest x7 9.95 us: over_pages(): return lax.psum(tensor.astype(HALF), 'page').astype(F32)]
    psum x2 -> x1, blocking collectives: 256 us -> 12 us  [over_pages(): return lax.psum(tensor.astype(HALF), 'page').astype(F32)]
    pallas_call x0 -> x8, Pallas kernels: none -> 182 us  [the longest x2 70.5 us: self_backward(): pl.pallas_call(partial(self_backward_kernel, n=n, n_heads=n_heads, head_d...]
    reduce_sum x32 -> x16, other arithmetic: 153 us -> 20.7 us  [the longest x11 16.7 us: col_sums(): return jnp.sum(tensor.astype(F32), axis=0)]
    reduce_scatter x8 -> x6, waiting for transfers between devices: 401 us -> 281 us  [scatter(): lax.psum_scatter(tensor.astype(HALF), 'blk', scatter_dimension=axis, tile...]
    ppermute x0 -> x56, waiting for transfers between devices: none -> 111 us  [swap(): return lax.ppermute(piece, 'blk', [(k, k ^ step) for k in range(n)])]
    all_gather x1 -> x0, waiting for transfers between devices: 111 us -> none  [shards(): kv_whole = lax.all_gather(key_val, 'blk', axis=1, tiled=True)]
  transfers between devices with their start and end apart: 14 -> 66, of which waited for: 8 -> 25; matrix products, arithmetic and copies ran while one was open for 10% -> 13% of each run, Pallas kernels for 0% -> 11%
where the time goes in v1:
time: 1120 us
  waiting for transfers between devices  554 us (49%)
  matrix products  190 us (17%)
  Pallas kernels  182 us (16%)
  starting transfers between devices  60.1 us (5%)
  local copies, waits for them, and re-layouts  57.3 us (5%)
  other arithmetic  50 us (4%)
  between operations  16.5 us (1%)
  blocking collectives  12 us (1%)
    reduce_scatter x6, waiting for transfers between devices, scatter(): lax.psum_scatter(tensor.astype(HALF), 'blk', scatter_dimension=axis, tile...  281 us
    dot_general x27, matrix products, mxu(): return lax.dot_general(left_op, right_op, dims, preferred_element_type=F32)  190 us
    psum x1, waiting for transfers between devices, over_pages(): return lax.psum(tensor.astype(HALF), 'page').astype(F32)  146 us
    ppermute x56, waiting for transfers between devices, swap(): return lax.ppermute(piece, 'blk', [(k, k ^ step) for k in range(n)])  111 us
    pallas_call x2, Pallas kernels, self_backward(): pl.pallas_call(partial(self_backward_kernel, n=n, n_heads=n_heads, head_d...  70.5 us
    ppermute x56, starting transfers between devices, swap(): return lax.ppermute(piece, 'blk', [(k, k ^ step) for k in range(n)])  59 us
    pallas_call x2, Pallas kernels, self_forward(): pl.pallas_call(partial(self_forward_kernel, n=n, n_heads=n_heads, head_di...  49.4 us
    pallas_call x2, Pallas kernels, cross_backward(): pl.pallas_call(partial(cross_backward_kernel, mem_count=mem_count, head_d...  35.4 us
  transfers between devices with their start and end apart: 66, of which 25 were waited for; matrix products, arithmetic and copies ran while one was open for 13% of the time, Pallas kernels for 11%

profile of v1, /device:TPU:0, one launch (start us, length us, event | category | flops | bytes accessed | tf_op | source)
XLA Modules:
  0.0 1121.5 jit_solution(10165442338321290802)
XLA Ops:
  11.7 8.7 copy.48
  20.4 6.5 copy.49
  29.5 7.2 multiply_convert_fusion.3
  44.1 4.2 convert_element_type.165
  48.4 6.1 multiply_convert_fusion.2
  77.6 9.4 collective-permute-done.6.refs_7_
  90.3 6.1 collective-permute-done.15.refs_2_
  96.8 39.6 %self_forward.2 = (bf16[512,128]{1,0:T(8,128)(2,1)}, bf16[512,128]{1,0:T(8,128)(2,1)}, bf16[512,128]{1,0:T(8,128)(2,1)}, bf16[512,128]{1,0:T(8,128)(2,1)}, bf16[...) custom-call(s32[2]{0:T(128)} %pad_add_fusion.scalars, ...), custom_call_target="tpu_custom_call" | custom-call | flops 8589934592 | bytes 5242880 | tf_op jit(solution)/shard_map/self_forward/pallas_call | solution.py:146
  141.5 9.8 self_forward.3
  167.7 4.5 collective-permute-done.24
  174.7 3.7 collective-permute-done.26
  193.2 5.2 fusion.71
  201.6 13.0 %cross_forward.2 = (bf16[512,1024]{1,0:T(8,128)(2,1)}, f32[8,2,512]{2,1,0:T(2,128)}) custom-call(s32[2]{0:T(128)} %pad_add_fusion.scalars, bf16[512,1024]{1,0:T(8,128)(2,1)} %multiply_convert_fusion.7.query_ref, bf16[592,1024]{1,0:T(8,128)(2,1)} %get-tuple-element.195.key_ref, bf16[592,1024]{1,0:T(8,128)(2,1)} %get-tuple-element.279.value_ref), custom_call_target="tpu_custom_call" | custom-call | flops 2483027968 | bytes 4521984 | tf_op jit(solution)/shard_map/cross_forward/pallas_call | solution.py:346
  216.9 13.5 %cross_forward.3 = (bf16[512,1024]{1,0:T(8,128)(2,1)}, f32[8,2,512]{2,1,0:T(2,128)}) custom-call(s32[2]{0:T(128)} %pad_add_fusion.1.scalars, bf16[512,1024]{1,0:T(8,128)(2,1)} %multiply_convert_fusion.6.query_ref, bf16[592,1024]{1,0:T(8,128)(2,1)} %get-tuple-element.194.key_ref, bf16[592,1024]{1,0:T(8,128)(2,1)} %get-tuple-element.280.value_ref), custom_call_target="tpu_custom_call" | custom-call | flops 2483027968 | bytes 4521984 | tf_op jit(solution)/shard_map/cross_forward/pallas_call | solution.py:346
  232.7 4.8 fusion.72
  238.3 16.9 %multiply_convert_fusion.1 = (bf16[1024,4096]{1,0:T(8,128)(2,1)}, f32[1024,4096]{1,0:T(8,128)}) fusion(f32[4096]{0:T(1024)S(1)} %copy-done.121, bf16[1024,4096]{1,0:T(8,128)(2,1)S(1)} %bitcast.178, f32[1024,1024]{1,0:T(8,128)S(1)} %get-tuple-element.269, f32[1024]{0:T(1024)S(1)} %bitcast.175, f32[1024]{0:T(1024)S(1)} %bitcast.162, ...), kind=kOutput, calls=%fused_computation.7 | convolution fusion | flops 8620343296 | bytes 37781504 | tf_op jit(solution)/shard_map/dot_general | solution.py:24
  255.2 19.3 %fusion.73 = (bf16[4096]{0:T(1024)(128)(2,1)}, bf16[1024,4096]{1,0:T(8,128)(2,1)}) fusion(bf16[1024,1024]{1,0:T(8,128)(2,1)S(1)} %copy-done.24, bf16[4096,1024]{1,0:T(8,128)(2,1)} %param.29, f32[1024,4096]{1,0:T(8,128)} %get-tuple-element.271, f32[4096]{0:T(1024)S(1)} %copy-done.121), kind=kOutput, calls=%fused_computation.221 | convolution fusion | flops 8648650752 | bytes 35676160 | tf_op jit(solution)/shard_map/dot_general | solution.py:24
  274.5 15.8 %multiply_reduce_fusion = (bf16[1024]{0:T(1024)(128)(2,1)}, f32[1024]{0:T(1024)S(1)}, f32[1024]{0:T(1024)S(1)}, bf16[1024]{0:T(1024)(128)(2,1)}, f32[1024,1024]{1,0:T(8,128)S(1)}) fusion(f32[1024,1024]{1,0:T(8,128)S(1)} %get-tuple-element.269, f32[1024]{0:T(1024)S(1)} %add_rsqrt_fusion, f32[1024]{0:T(1024)S(1)} %broadcast_multiply_fusion.4, ...), kind=kOutput, calls=%fused_computation.28 | convolution fusion | flops 8599367680 | bytes 25190400 | tf_op jit(solution)/shard_map/dot_general | solution.py:24
  298.3 17.4 %cross_backward.3 = (bf16[512,1024]{1,0:T(8,128)(2,1)}, bf16[592,1024]{1,0:T(8,128)(2,1)}, bf16[592,1024]{1,0:T(8,128)(2,1)}) custom-call(s32[2]{0:T(128)} %pad_add_fusion.1.scalars, bf16[512,1024]{1,0:T(8,128)(2,1)} %multiply_convert_fusion.6.query_ref, bf16[592,1024]{1,0:T(8,128)(2,1)} %get-tuple-element.194.key_ref, ...), custom_call_target="tpu_custom_call" | custom-call | flops 6207569920 | bytes 11304960 | tf_op jit(solution)/shard_map/cross_backward/pallas_call | solution.py:425
  315.8 3.8 fusion.74
  319.6 18.0 %cross_backward.2 = (bf16[512,1024]{1,0:T(8,128)(2,1)}, bf16[592,1024]{1,0:T(8,128)(2,1)}, bf16[592,1024]{1,0:T(8,128)(2,1)}) custom-call(s32[2]{0:T(128)} %pad_add_fusion.scalars, bf16[512,1024]{1,0:T(8,128)(2,1)} %multiply_convert_fusion.7.query_ref, bf16[592,1024]{1,0:T(8,128)(2,1)} %get-tuple-element.195.key_ref, ...), custom_call_target="tpu_custom_call" | custom-call | flops 6207569920 | bytes 11304960 | tf_op jit(solution)/shard_map/cross_backward/pallas_call | solution.py:425
  337.7 4.9 multiply_reduce_fusion.9
  368.6 61.4 %self_backward.2 = (bf16[512,384]{1,0:T(8,128)(2,1)}, bf16[512,384]{1,0:T(8,128)(2,1)}, bf16[512,384]{1,0:T(8,128)(2,1)}, bf16[512,384]{1,0:T(8,128)(2,1)}, bf16...) custom-call(s32[2]{0:T(128)} %pad_add_fusion.scalars, ...), custom_call_target="tpu_custom_call" | custom-call | flops 10737418240 | bytes 10485760 | tf_op jit(solution)/shard_map/self_backward/pallas_call | solution.py:268
  434.5 9.2 self_backward.3
  448.7 8.7 collective-permute-done.37
  460.2 10.9 collective-permute-done.39
  471.1 3.8 collective-permute-start.51
  475.2 10.5 collective-permute-done.41
  488.0 14.1 %collective-permute-done.50 = bf16[512,384]{1,0:T(8,128)(2,1)S(1)} collective-permute-done((bf16[512,384]{1,0:T(8,128)(2,1)S(1)}, bf16[512,384]{1,0:T(8,128)(2,1)S(1)}, u32[]{:S(2)}, u32[]{:S(2)}) %collective-permute-start.50) | collective-permute-done | bytes 393248 | tf_op jit(solution)/shard_map/ppermute | solution.py:467
  502.3 8.3 collective-permute-done.51
  510.8 18.1 %collective-permute-done.53 = bf16[512,384]{1,0:T(8,128)(2,1)S(1)} collective-permute-done((bf16[512,384]{1,0:T(8,128)(2,1)S(1)}, bf16[512,384]{1,0:T(8,128)(2,1)S(1)}, u32[]{:S(2)}, u32[]{:S(2)}) %collective-permute-start.53) | collective-permute-done | bytes 393248 | tf_op jit(solution)/shard_map/ppermute | solution.py:467
  530.9 9.0 convolution_convert_fusion.2
  541.4 5.2 fusion.32
  546.8 5.7 fusion.37
  552.6 5.3 convolution_convert_fusion.3
  558.0 16.0 %convolution_convert_fusion.1 = bf16[1024,4096]{1,0:T(8,128)(2,1)} fusion(bf16[1024,4096]{1,0:T(8,128)(2,1)} %get-tuple-element.276, f32[1024,1024]{1,0:T(8,128)} %copy-done.12, f32[1024]{0:T(1024)S(1)} %bitcast.176, f32[1024]{0:T(1024)S(1)} %bitcast.165, f32[1024]{0:T(1024)S(1)} %add_rsqrt_fusion, f32[1024]{0:T(1024)S(1)} %broadcast_multiply_fusion.4), kind=kOutput, calls=%fused_computation.10 | convolution fusion | flops 8599371776 | bytes 20987904 | tf_op jit(solution)/shard_map/dot_general | solution.py:24
  575.6 14.6 %convolution_convert_fusion = bf16[4096,1024]{1,0:T(8,128)(2,1)} fusion(bf16[1024,4096]{1,0:T(8,128)(2,1)} %get-tuple-element.270, bf16[1024,1024]{1,0:T(8,128)(2,1)S(1)} %copy-done.25), kind=kOutput, calls=%fused_computation.9 | convolution fusion | flops 8594128896 | bytes 18874368 | tf_op jit(solution)/shard_map/dot_general | solution.py:24
  599.5 13.8 %multiply_reduce_fusion.1 = (bf16[1024]{0:T(1024)(128)(2,1)S(1)}, f32[1024]{0:T(1024)S(1)}, f32[1024]{0:T(1024)S(1)}, bf16[1024]{0:T(1024)(128)(2,1)S(1)}, f32[1024,1024]{1,0:T(8,128)}) fusion(bf16[2,512,1024]{2,1,0:T(8,128)(2,1)S(1)} %copy-done.3, f32[1024]{0:T(1024)S(1)} %bitcast.151, f32[1024]{0:T(1024)S(1)} %bitcast.154, f32[1024]{0:T(1024)S(1)} %bitcast.157, ...), kind=kOutput, calls=%fused_computation.29 | convolution fusion | flops 6465515520 | bytes 18898944 | tf_op jit(solution)/shard_map/dot_general | solution.py:24
  617.0 4.1 fusion.12
  623.6 41.6 %reduce-scatter.14.cloned.1.call-done = bf16[128,1024]{1,0:T(8,128)(2,1)} async-done(((bf16[1024,1024]{1,0:T(8,128)(2,1)}), bf16[128,1024]{1,0:T(8,128)(2,1)}) %reduce-scatter.14.cloned.1.call-update) | async-done | bytes 262160 | tf_op jit(solution)/shard_map/reduce_scatter | solution.py:678
  665.3 45.3 %reduce-scatter.12.cloned.1.call-done = bf16[128,1024]{1,0:T(8,128)(2,1)} async-done(((bf16[1024,1024]{1,0:T(8,128)(2,1)}), bf16[128,1024]{1,0:T(8,128)(2,1)}) %reduce-scatter.12.cloned.1.call-update) | async-done | bytes 262160 | tf_op jit(solution)/shard_map/reduce_scatter | solution.py:678
  710.6 44.4 %reduce-scatter.16.cloned.1.call-done = bf16[128,1024]{1,0:T(8,128)(2,1)} async-done(((bf16[1024,1024]{1,0:T(8,128)(2,1)}), bf16[128,1024]{1,0:T(8,128)(2,1)}) %reduce-scatter.16.cloned.1.call-update) | async-done | bytes 262160 | tf_op jit(solution)/shard_map/reduce_scatter | solution.py:678
  755.0 75.2 %reduce-scatter.18.cloned.1.call-done = bf16[128,4096]{1,0:T(8,128)(2,1)} async-done(((bf16[1024,4096]{1,0:T(8,128)(2,1)}), bf16[128,4096]{1,0:T(8,128)(2,1)}) %reduce-scatter.18.cloned.1.call-update) | async-done | bytes 1048592 | tf_op jit(solution)/shard_map/reduce_scatter | solution.py:678
  830.2 74.7 %reduce-scatter.20.cloned.1.call-done = bf16[512,1024]{1,0:T(8,128)(2,1)} async-done(((bf16[4096,1024]{1,0:T(8,128)(2,1)}), bf16[512,1024]{1,0:T(8,128)(2,1)}) %reduce-scatter.20.cloned.1.call-update) | async-done | bytes 1048592 | tf_op jit(solution)/shard_map/reduce_scatter | solution.py:678
  905.0 15.4 %multiply_convert_fusion.5 = bf16[1024,1024]{1,0:T(8,128)(2,1)} fusion(f32[1024,1024]{1,0:T(8,128)} %copy-done.12, f32[1024]{0:T(1024)S(1)} %bitcast.146, f32[1024]{0:T(1024)S(1)} %bitcast.169, bf16[1024,4096]{1,0:T(8,128)(2,1)} %get-tuple-element.270, bf16[4096,1024]{1,0:T(8,128)(2,1)} %param.29), kind=kOutput, calls=%fused_computation.33 | convolution fusion | flops 8594128896 | bytes 23076864 | tf_op jit(solution)/shard_map/dot_general | solution.py:24
  927.4 15.1 %reduce-scatter.22.cloned.1.call-done = bf16[128,17]{1,0:T(8,128)(2,1)} async-done(((bf16[1024,17]{1,0:T(8,128)(2,1)}), bf16[128,17]{1,0:T(8,128)(2,1)}) %reduce-scatter.22.cloned.1.call-update) | async-done | bytes 4368
  943.3 12.0 %psum.64 = bf16[17,128]{1,0:T(8,128)(2,1)S(1)} all-reduce(bf16[17,128]{1,0:T(8,128)(2,1)S(1)} %copy.58), channel_id=1, replica_groups=mesh['page'=4,'blk'=8] {'page'}, use_global_device_ids=true, to_apply=%region_33.34 | all-reduce | flops 2176 | bytes 8704 | tf_op jit(solution)/shard_map/psum | solution.py:681
  957.0 146.0 %all-reduce.8.cloned.1.call-done = (bf16[128,3072]{0,1:T(8,128)(2,1)}, bf16[128,1024]{1,0:T(8,128)(2,1)}, bf16[128,1024]{1,0:T(8,128)(2,1)}, bf16[128,2048]{1,0:...) async-done(((bf16[128,3072]{0,1:T(8,128)(2,1)}, bf16[128,1024]{1,0:T(8,128)(2,1)}, bf16[128,1024]{1,0:T(8,128)(2,1)}, ...) | async-done | bytes 4194320 | tf_op jit(solution)/shard_map/psum | solution.py:681
  (524 shorter events, 178.0 us)
Async XLA Ops:
  7.2 183.1 %all-gather.2.cloned.1.call-start = ((), (), s32[]{:S(2)}) async-start(), calls=%async_computation.7 | async-start | bytes 2727936 | tf_op jit(solution)/shard_map/all_gather | solution.py:552
  38.2 21.9 %collective-permute-start = (bf16[512,384]{1,0:T(8,128)(2,1)}, bf16[512,384]{1,0:T(8,128)(2,1)}, u32[]{:S(2)}, u32[]{:S(2)}) collective-permute-start(bf16[512,384]{1,0:T(8,128)(2,1)} %get-tuple-element.205), channel_id=1, source_target_pairs={{0,1},{1,0},{2,3},{3,2},{4,5},{5,4},{6,7},{7,6},{8,9},{9,8},{10,11... | collective-permute-start | bytes 1179656 | tf_op jit(solution)/shard_map/ppermute | solution.py:467
  38.6 24.0 %collective-permute-start.1 = (bf16[512,384]{1,0:T(8,128)(2,1)}, bf16[512,384]{1,0:T(8,128)(2,1)}, u32[]{:S(2)}, u32[]{:S(2)}) collective-permute-start(bf16[512,384]{1,0:T(8,128)(2,1)} %get-tuple-element.204), channel_id=1, source_target_pairs={{0,2},{1,3},{2,0},{3,1},{4,6},{5,7},{6,4},{7,5},{8,10},{9,11},{10,... | collective-permute-start | bytes 1179656 | tf_op jit(solution)/shard_map/ppermute | solution.py:467
  41.1 21.7 %collective-permute-start.2 = (bf16[512,384]{1,0:T(8,128)(2,1)}, bf16[512,384]{1,0:T(8,128)(2,1)}, u32[]{:S(2)}, u32[]{:S(2)}) collective-permute-start(bf16[512,384]{1,0:T(8,128)(2,1)} %get-tuple-element.203), channel_id=1, source_target_pairs={{0,3},{1,2},{2,1},{3,0},{4,7},{5,6},{6,5},{7,4},{8,11},{9,10},{10,... | collective-permute-start | bytes 1179656 | tf_op jit(solution)/shard_map/ppermute | solution.py:467
  41.3 21.9 %collective-permute-start.3 = (bf16[512,384]{1,0:T(8,128)(2,1)}, bf16[512,384]{1,0:T(8,128)(2,1)}, u32[]{:S(2)}, u32[]{:S(2)}) collective-permute-start(bf16[512,384]{1,0:T(8,128)(2,1)} %get-tuple-element.202), channel_id=1, source_target_pairs={{0,4},{1,5},{2,6},{3,7},{4,0},{5,1},{6,2},{7,3},{8,12},{9,13},{10,... | collective-permute-start | bytes 1179656 | tf_op jit(solution)/shard_map/ppermute | solution.py:467
  43.0 27.6 %collective-permute-start.4 = (bf16[512,384]{1,0:T(8,128)(2,1)S(1)}, bf16[512,384]{1,0:T(8,128)(2,1)}, u32[]{:S(2)}, u32[]{:S(2)}) collective-permute-start(bf16[512,384]{1,0:T(8,128)(2,1)S(1)} %get-tuple-element.201), channel_id=1, source_target_pairs={{0,5},{1,4},{2,7},{3,6},{4,1},{5,0},{6,3},{7,2},{8,13},{9,12},{10,... | collective-permute-start | bytes 1179656 | tf_op jit(solution)/shard_map/ppermute | solution.py:467
  43.8 569.6 %all-reduce.6.cloned.1.call-start = ((), (), s32[]{:S(2)}) async-start(), calls=%async_computation.8 | async-start | bytes 9699328 | tf_op jit(solution)/shard_map/psum | solution.py:644
  62.6 24.4 %collective-permute-start.6 = (bf16[512,384]{1,0:T(8,128)(2,1)S(1)}, bf16[512,384]{1,0:T(8,128)(2,1)S(1)}, u32[]{:S(2)}, u32[]{:S(2)}) collective-permute-start(bf16[512,384]{1,0:T(8,128)(2,1)S(1)} %get-tuple-element.199), channel_id=1, source_target_pairs={{0,7},{1,6},{2,5},{3,4},{4,3},{5,2},{6,1},{7,0},{8,15},{9,14},{10,... | collective-permute-start | bytes 1179656 | tf_op jit(solution)/shard_map/ppermute | solution.py:467
  62.8 26.1 %collective-permute-start.14 = (bf16[512,384]{1,0:T(8,128)(2,1)S(1)}, bf16[512,384]{1,0:T(8,128)(2,1)S(1)}, u32[]{:S(2)}, u32[]{:S(2)}) collective-permute-start(bf16[512,384]{1,0:T(8,128)(2,1)S(1)} %get-tuple-element.213), channel_id=1, source_target_pairs={{0,1},{1,0},{2,3},{3,2},{4,5},{5,4},{6,7},{7,6},{8,9},{9,8},{10,11... | collective-permute-start | bytes 1179656 | tf_op jit(solution)/shard_map/ppermute | solution.py:467
  63.1 33.3 %collective-permute-start.15 = (bf16[512,384]{1,0:T(8,128)(2,1)S(1)}, bf16[512,384]{1,0:T(8,128)(2,1)S(1)}, u32[]{:S(2)}, u32[]{:S(2)}) collective-permute-start(bf16[512,384]{1,0:T(8,128)(2,1)S(1)} %get-tuple-element.212), channel_id=1, source_target_pairs={{0,2},{1,3},{2,0},{3,1},{4,6},{5,7},{6,4},{7,5},{8,10},{9,11},{10,... | collective-permute-start | bytes 1179656 | tf_op jit(solution)/shard_map/ppermute | solution.py:467
  70.6 65.8 %collective-permute-start.16 = (bf16[512,384]{1,0:T(8,128)(2,1)S(1)}, bf16[512,384]{1,0:T(8,128)(2,1)S(1)}, u32[]{:S(2)}, u32[]{:S(2)}) collective-permute-start(bf16[512,384]{1,0:T(8,128)(2,1)S(1)} %get-tuple-element.211), channel_id=1, source_target_pairs={{0,3},{1,2},{2,1},{3,0},{4,7},{5,6},{6,5},{7,4},{8,11},{9,10},{10,... | collective-permute-start | bytes 1179656 | tf_op jit(solution)/shard_map/ppermute | solution.py:467
  76.3 61.5 %collective-permute-start.17 = (bf16[512,384]{1,0:T(8,128)(2,1)S(1)}, bf16[512,384]{1,0:T(8,128)(2,1)S(1)}, u32[]{:S(2)}, u32[]{:S(2)}) collective-permute-start(bf16[512,384]{1,0:T(8,128)(2,1)S(1)} %get-tuple-element.210), channel_id=1, source_target_pairs={{0,4},{1,5},{2,6},{3,7},{4,0},{5,1},{6,2},{7,3},{8,12},{9,13},{10,... | collective-permute-start | bytes 1179656 | tf_op jit(solution)/shard_map/ppermute | solution.py:467
  87.0 51.2 %collective-permute-start.18 = (bf16[512,384]{1,0:T(8,128)(2,1)S(1)}, bf16[512,384]{1,0:T(8,128)(2,1)S(1)}, u32[]{:S(2)}, u32[]{:S(2)}) collective-permute-start(bf16[512,384]{1,0:T(8,128)(2,1)S(1)} %get-tuple-element.209), channel_id=1, source_target_pairs={{0,5},{1,4},{2,7},{3,6},{4,1},{5,0},{6,3},{7,2},{8,13},{9,12},{10,... | collective-permute-start | bytes 1179656 | tf_op jit(solution)/shard_map/ppermute | solution.py:467
  88.9 50.3 %collective-permute-start.19 = (bf16[512,384]{1,0:T(8,128)(2,1)S(1)}, bf16[512,384]{1,0:T(8,128)(2,1)S(1)}, u32[]{:S(2)}, u32[]{:S(2)}) collective-permute-start(bf16[512,384]{1,0:T(8,128)(2,1)S(1)} %get-tuple-element.208), channel_id=1, source_target_pairs={{0,6},{1,7},{2,4},{3,5},{4,2},{5,3},{6,0},{7,1},{8,14},{9,15},{10,... | collective-permute-start | bytes 1179656 | tf_op jit(solution)/shard_map/ppermute | solution.py:467
  96.4 44.3 %collective-permute-start.20 = (bf16[512,384]{1,0:T(8,128)(2,1)S(1)}, bf16[512,384]{1,0:T(8,128)(2,1)S(1)}, u32[]{:S(2)}, u32[]{:S(2)}) collective-permute-start(bf16[512,384]{1,0:T(8,128)(2,1)S(1)} %get-tuple-element.207), channel_id=1, source_target_pairs={{0,7},{1,6},{2,5},{3,4},{4,3},{5,2},{6,1},{7,0},{8,15},{9,14},{10,... | collective-permute-start | bytes 1179656 | tf_op jit(solution)/shard_map/ppermute | solution.py:467
  136.5 16.7 %collective-permute-start.7 = (bf16[512,128]{1,0:T(8,128)(2,1)}, bf16[512,128]{1,0:T(8,128)(2,1)S(1)}, u32[]{:S(2)}, u32[]{:S(2)}) collective-permute-start(bf16[512,128]{1,0:T(8,128)(2,1)} %get-tuple-element.61), channel_id=1, source_target_pairs={{0,1},{1,0},{2,3},{3,2},{4,5},{5,4},{6,7},{7,6},{8,9},{9,8},{10,11... | collective-permute-start | bytes 393224 | tf_op jit(solution)/shard_map/ppermute | solution.py:467
  137.7 16.6 %collective-permute-start.8 = (bf16[512,128]{1,0:T(8,128)(2,1)}, bf16[512,128]{1,0:T(8,128)(2,1)S(1)}, u32[]{:S(2)}, u32[]{:S(2)}) collective-permute-start(bf16[512,128]{1,0:T(8,128)(2,1)} %get-tuple-element.62), channel_id=1, source_target_pairs={{0,2},{1,3},{2,0},{3,1},{4,6},{5,7},{6,4},{7,5},{8,10},{9,11},{10,... | collective-permute-start | bytes 393224 | tf_op jit(solution)/shard_map/ppermute | solution.py:467
  138.2 21.9 %collective-permute-start.9 = (bf16[512,128]{1,0:T(8,128)(2,1)}, bf16[512,128]{1,0:T(8,128)(2,1)S(1)}, u32[]{:S(2)}, u32[]{:S(2)}) collective-permute-start(bf16[512,128]{1,0:T(8,128)(2,1)} %get-tuple-element.63), channel_id=1, source_target_pairs={{0,3},{1,2},{2,1},{3,0},{4,7},{5,6},{6,5},{7,4},{8,11},{9,10},{10,... | collective-permute-start | bytes 393224 | tf_op jit(solution)/shard_map/ppermute | solution.py:467
  139.2 28.4 %collective-permute-start.10 = (bf16[512,128]{1,0:T(8,128)(2,1)}, bf16[512,128]{1,0:T(8,128)(2,1)S(1)}, u32[]{:S(2)}, u32[]{:S(2)}) collective-permute-start(bf16[512,128]{1,0:T(8,128)(2,1)} %get-tuple-element.64), channel_id=1, source_target_pairs={{0,4},{1,5},{2,6},{3,7},{4,0},{5,1},{6,2},{7,3},{8,12},{9,13},{10,... | collective-permute-start | bytes 393224 | tf_op jit(solution)/shard_map/ppermute | solution.py:467
  153.2 21.2 %collective-permute-start.11 = (bf16[512,128]{1,0:T(8,128)(2,1)S(1)}, bf16[512,128]{1,0:T(8,128)(2,1)S(1)}, u32[]{:S(2)}, u32[]{:S(2)}) collective-permute-start(bf16[512,128]{1,0:T(8,128)(2,1)S(1)} %copy-done.108), channel_id=1, source_target_pairs={{0,5},{1,4},{2,7},{3,6},{4,1},{5,0},{6,3},{7,2},{8,13},{9,12},{10,... | collective-permute-start | bytes 393224 | tf_op jit(solution)/shard_map/ppermute | solution.py:467
  154.3 20.3 %collective-permute-start.12 = (bf16[512,128]{1,0:T(8,128)(2,1)S(1)}, bf16[512,128]{1,0:T(8,128)(2,1)S(1)}, u32[]{:S(2)}, u32[]{:S(2)}) collective-permute-start(bf16[512,128]{1,0:T(8,128)(2,1)S(1)} %copy-done.106), channel_id=1, source_target_pairs={{0,6},{1,7},{2,4},{3,5},{4,2},{5,3},{6,0},{7,1},{8,14},{9,15},{10,... | collective-permute-start | bytes 393224 | tf_op jit(solution)/shard_map/ppermute | solution.py:467
  160.2 18.3 %collective-permute-start.13 = (bf16[512,128]{1,0:T(8,128)(2,1)S(1)}, bf16[512,128]{1,0:T(8,128)(2,1)S(1)}, u32[]{:S(2)}, u32[]{:S(2)}) collective-permute-start(bf16[512,128]{1,0:T(8,128)(2,1)S(1)} %copy-done.105), channel_id=1, source_target_pairs={{0,7},{1,6},{2,5},{3,4},{4,3},{5,2},{6,1},{7,0},{8,15},{9,14},{10,... | collective-permute-start | bytes 393224 | tf_op jit(solution)/shard_map/ppermute | solution.py:467
  362.1 259.1 %reduce-scatter.10.cloned.1.call-start = ((), (), s32[]{:S(2)}) async-start(), calls=%async_computation.9 | async-start | bytes 7077888 | tf_op jit(solution)/shard_map/reduce_scatter | solution.py:678
  362.2 67.8 %collective-permute-start.44 = (bf16[512,128]{1,0:T(8,128)(2,1)S(1)}, bf16[512,128]{1,0:T(8,128)(2,1)S(1)}, u32[]{:S(2)}, u32[]{:S(2)}) collective-permute-start(bf16[512,128]{1,0:T(8,128)(2,1)S(1)} %get-tuple-element.229), channel_id=1, source_target_pairs={{0,3},{1,2},{2,1},{3,0},{4,7},{5,6},{6,5},{7,4},{8,11},{9,10},{10,... | collective-permute-start | bytes 393224 | tf_op jit(solution)/shard_map/ppermute | solution.py:467
  363.7 67.2 %collective-permute-start.45 = (bf16[512,128]{1,0:T(8,128)(2,1)S(1)}, bf16[512,128]{1,0:T(8,128)(2,1)S(1)}, u32[]{:S(2)}, u32[]{:S(2)}) collective-permute-start(bf16[512,128]{1,0:T(8,128)(2,1)S(1)} %get-tuple-element.228), channel_id=1, source_target_pairs={{0,4},{1,5},{2,6},{3,7},{4,0},{5,1},{6,2},{7,3},{8,12},{9,13},{10,... | collective-permute-start | bytes 393224 | tf_op jit(solution)/shard_map/ppermute | solution.py:467
  365.6 67.1 %collective-permute-start.46 = (bf16[512,128]{1,0:T(8,128)(2,1)S(1)}, bf16[512,128]{1,0:T(8,128)(2,1)S(1)}, u32[]{:S(2)}, u32[]{:S(2)}) collective-permute-start(bf16[512,128]{1,0:T(8,128)(2,1)S(1)} %get-tuple-element.227), channel_id=1, source_target_pairs={{0,5},{1,4},{2,7},{3,6},{4,1},{5,0},{6,3},{7,2},{8,13},{9,12},{10,... | collective-permute-start | bytes 393224 | tf_op jit(solution)/shard_map/ppermute | solution.py:467
  366.3 66.5 %collective-permute-start.47 = (bf16[512,128]{1,0:T(8,128)(2,1)S(1)}, bf16[512,128]{1,0:T(8,128)(2,1)S(1)}, u32[]{:S(2)}, u32[]{:S(2)}) collective-permute-start(bf16[512,128]{1,0:T(8,128)(2,1)S(1)} %get-tuple-element.226), channel_id=1, source_target_pairs={{0,6},{1,7},{2,4},{3,5},{4,2},{5,3},{6,0},{7,1},{8,14},{9,15},{10,... | collective-permute-start | bytes 393224 | tf_op jit(solution)/shard_map/ppermute | solution.py:467
  368.1 65.8 %collective-permute-start.48 = (bf16[512,128]{1,0:T(8,128)(2,1)S(1)}, bf16[512,128]{1,0:T(8,128)(2,1)S(1)}, u32[]{:S(2)}, u32[]{:S(2)}) collective-permute-start(bf16[512,128]{1,0:T(8,128)(2,1)S(1)} %get-tuple-element.225), channel_id=1, source_target_pairs={{0,7},{1,6},{2,5},{3,4},{4,3},{5,2},{6,1},{7,0},{8,15},{9,14},{10,... | collective-permute-start | bytes 393224 | tf_op jit(solution)/shard_map/ppermute | solution.py:467
  430.9 16.7 %collective-permute-start.36 = (bf16[512,384]{1,0:T(8,128)(2,1)}, bf16[512,384]{1,0:T(8,128)(2,1)S(1)}, u32[]{:S(2)}, u32[]{:S(2)}) collective-permute-start(bf16[512,384]{1,0:T(8,128)(2,1)} %get-tuple-element.86), channel_id=1, source_target_pairs={{0,2},{1,3},{2,0},{3,1},{4,6},{5,7},{6,4},{7,5},{8,10},{9,11},{10,... | collective-permute-start | bytes 1179656 | tf_op jit(solution)/shard_map/ppermute | solution.py:467
  432.7 24.7 %collective-permute-start.37 = (bf16[512,384]{1,0:T(8,128)(2,1)}, bf16[512,384]{1,0:T(8,128)(2,1)S(1)}, u32[]{:S(2)}, u32[]{:S(2)}) collective-permute-start(bf16[512,384]{1,0:T(8,128)(2,1)} %get-tuple-element.87), channel_id=1, source_target_pairs={{0,3},{1,2},{2,1},{3,0},{4,7},{5,6},{6,5},{7,4},{8,11},{9,10},{10,... | collective-permute-start | bytes 1179656 | tf_op jit(solution)/shard_map/ppermute | solution.py:467
  432.8 25.4 %collective-permute-start.38 = (bf16[512,384]{1,0:T(8,128)(2,1)}, bf16[512,384]{1,0:T(8,128)(2,1)S(1)}, u32[]{:S(2)}, u32[]{:S(2)}) collective-permute-start(bf16[512,384]{1,0:T(8,128)(2,1)} %get-tuple-element.88), channel_id=1, source_target_pairs={{0,4},{1,5},{2,6},{3,7},{4,0},{5,1},{6,2},{7,3},{8,12},{9,13},{10,... | collective-permute-start | bytes 1179656 | tf_op jit(solution)/shard_map/ppermute | solution.py:467
  433.9 37.3 %collective-permute-start.39 = (bf16[512,384]{1,0:T(8,128)(2,1)}, bf16[512,384]{1,0:T(8,128)(2,1)S(1)}, u32[]{:S(2)}, u32[]{:S(2)}) collective-permute-start(bf16[512,384]{1,0:T(8,128)(2,1)} %get-tuple-element.89), channel_id=1, source_target_pairs={{0,5},{1,4},{2,7},{3,6},{4,1},{5,0},{6,3},{7,2},{8,13},{9,12},{10,... | collective-permute-start | bytes 1179656 | tf_op jit(solution)/shard_map/ppermute | solution.py:467
  445.7 29.3 %collective-permute-start.40 = (bf16[512,384]{1,0:T(8,128)(2,1)S(1)}, bf16[512,384]{1,0:T(8,128)(2,1)S(1)}, u32[]{:S(2)}, u32[]{:S(2)}) collective-permute-start(bf16[512,384]{1,0:T(8,128)(2,1)S(1)} %copy-done.99), channel_id=1, source_target_pairs={{0,6},{1,7},{2,4},{3,5},{4,2},{5,3},{6,0},{7,1},{8,14},{9,15},{10,... | collective-permute-start | bytes 1179656 | tf_op jit(solution)/shard_map/ppermute | solution.py:467
  447.6 38.1 %collective-permute-start.41 = (bf16[512,384]{1,0:T(8,128)(2,1)S(1)}, bf16[512,384]{1,0:T(8,128)(2,1)S(1)}, u32[]{:S(2)}, u32[]{:S(2)}) collective-permute-start(bf16[512,384]{1,0:T(8,128)(2,1)S(1)} %copy-done.96), channel_id=1, source_target_pairs={{0,7},{1,6},{2,5},{3,4},{4,3},{5,2},{6,1},{7,0},{8,15},{9,14},{10,... | collective-permute-start | bytes 1179656 | tf_op jit(solution)/shard_map/ppermute | solution.py:467
  457.4 28.5 %collective-permute-start.49 = (bf16[512,384]{1,0:T(8,128)(2,1)S(1)}, bf16[512,384]{1,0:T(8,128)(2,1)S(1)}, u32[]{:S(2)}, u32[]{:S(2)}) collective-permute-start(bf16[512,384]{1,0:T(8,128)(2,1)S(1)} %copy-done.104), channel_id=1, source_target_pairs={{0,1},{1,0},{2,3},{3,2},{4,5},{5,4},{6,7},{7,6},{8,9},{9,8},{10,11... | collective-permute-start | bytes 1179656 | tf_op jit(solution)/shard_map/ppermute | solution.py:467
  458.2 43.9 %collective-permute-start.50 = (bf16[512,384]{1,0:T(8,128)(2,1)S(1)}, bf16[512,384]{1,0:T(8,128)(2,1)S(1)}, u32[]{:S(2)}, u32[]{:S(2)}) collective-permute-start(bf16[512,384]{1,0:T(8,128)(2,1)S(1)} %copy-done.103), channel_id=1, source_target_pairs={{0,2},{1,3},{2,0},{3,1},{4,6},{5,7},{6,4},{7,5},{8,10},{9,11},{10,... | collective-permute-start | bytes 1179656 | tf_op jit(solution)/shard_map/ppermute | solution.py:467
  471.1 39.4 %collective-permute-start.51 = (bf16[512,384]{1,0:T(8,128)(2,1)S(1)}, bf16[512,384]{1,0:T(8,128)(2,1)S(1)}, u32[]{:S(2)}, u32[]{:S(2)}) collective-permute-start(bf16[512,384]{1,0:T(8,128)(2,1)S(1)} %copy-done.102), channel_id=1, source_target_pairs={{0,3},{1,2},{2,1},{3,0},{4,7},{5,6},{6,5},{7,4},{8,11},{9,10},{10,... | collective-permute-start | bytes 1179656 | tf_op jit(solution)/shard_map/ppermute | solution.py:467
  475.1 35.6 %collective-permute-start.52 = (bf16[512,384]{1,0:T(8,128)(2,1)S(1)}, bf16[512,384]{1,0:T(8,128)(2,1)S(1)}, u32[]{:S(2)}, u32[]{:S(2)}) collective-permute-start(bf16[512,384]{1,0:T(8,128)(2,1)S(1)} %copy-done.101), channel_id=1, source_target_pairs={{0,4},{1,5},{2,6},{3,7},{4,0},{5,1},{6,2},{7,3},{8,12},{9,13},{10,... | collective-permute-start | bytes 1179656 | tf_op jit(solution)/shard_map/ppermute | solution.py:467
  485.7 43.2 %collective-permute-start.53 = (bf16[512,384]{1,0:T(8,128)(2,1)S(1)}, bf16[512,384]{1,0:T(8,128)(2,1)S(1)}, u32[]{:S(2)}, u32[]{:S(2)}) collective-permute-start(bf16[512,384]{1,0:T(8,128)(2,1)S(1)} %copy-done.100), channel_id=1, source_target_pairs={{0,5},{1,4},{2,7},{3,6},{4,1},{5,0},{6,3},{7,2},{8,13},{9,12},{10,... | collective-permute-start | bytes 1179656 | tf_op jit(solution)/shard_map/ppermute | solution.py:467
  485.9 43.0 %collective-permute-start.54 = (bf16[512,384]{1,0:T(8,128)(2,1)S(1)}, bf16[512,384]{1,0:T(8,128)(2,1)S(1)}, u32[]{:S(2)}, u32[]{:S(2)}) collective-permute-start(bf16[512,384]{1,0:T(8,128)(2,1)S(1)} %copy-done.98), channel_id=1, source_target_pairs={{0,6},{1,7},{2,4},{3,5},{4,2},{5,3},{6,0},{7,1},{8,14},{9,15},{10,... | collective-permute-start | bytes 1179656 | tf_op jit(solution)/shard_map/ppermute | solution.py:467
  502.2 26.9 %collective-permute-start.55 = (bf16[512,384]{1,0:T(8,128)(2,1)S(1)}, bf16[512,384]{1,0:T(8,128)(2,1)S(1)}, u32[]{:S(2)}, u32[]{:S(2)}) collective-permute-start(bf16[512,384]{1,0:T(8,128)(2,1)S(1)} %copy-done.97), channel_id=1, source_target_pairs={{0,7},{1,6},{2,5},{3,4},{4,3},{5,2},{6,1},{7,0},{8,15},{9,14},{10,... | collective-permute-start | bytes 1179656 | tf_op jit(solution)/shard_map/ppermute | solution.py:467
  539.9 125.4 %reduce-scatter.14.cloned.1.call-start = ((), (), s32[]{:S(2)}) async-start(), calls=%async_computation.11 | async-start | bytes 2359296 | tf_op jit(solution)/shard_map/reduce_scatter | solution.py:678
  546.7 163.9 %reduce-scatter.12.cloned.1.call-start = ((), (), s32[]{:S(2)}) async-start(), calls=%async_computation.10 | async-start | bytes 2359296 | tf_op jit(solution)/shard_map/reduce_scatter | solution.py:678
  552.5 202.5 %reduce-scatter.16.cloned.1.call-start = ((), (), s32[]{:S(2)}) async-start(), calls=%async_computation.12 | async-start | bytes 2359296 | tf_op jit(solution)/shard_map/reduce_scatter | solution.py:678
  557.9 272.2 %reduce-scatter.18.cloned.1.call-start = ((), (), s32[]{:S(2)}) async-start(), calls=%async_computation.13 | async-start | bytes 9437184 | tf_op jit(solution)/shard_map/reduce_scatter | solution.py:678
  574.0 330.9 %reduce-scatter.20.cloned.1.call-start = ((), (), s32[]{:S(2)}) async-start(), calls=%async_computation.14 | async-start | bytes 9437184 | tf_op jit(solution)/shard_map/reduce_scatter | solution.py:678
  590.3 352.1 %reduce-scatter.22.cloned.1.call-start = ((), (), s32[]{:S(2)}) async-start(), calls=%async_computation.15 | async-start | bytes 294912
  616.8 486.2 %all-reduce.8.cloned.1.call-start = ((), (), s32[]{:S(2)}) async-start(), calls=%async_computation.16 | async-start | bytes 8388608 | tf_op jit(solution)/shard_map/psum | solution.py:681
  (146 other events, 2629.4 us)
Sparse Core Ops, SparseCore 0:
  44.0 49.2 all-gather.1
  362.2 164.5 all-reduce.5
  540.0 80.2 reduce-scatter.9
  624.1 41.1 reduce-scatter.13
  669.3 41.2 reduce-scatter.11
  713.7 41.1 reduce-scatter.15
  758.8 71.2 reduce-scatter.17
  833.6 71.2 reduce-scatter.19
  908.8 33.5 reduce-scatter.21
  945.8 157.2 all-reduce.7
